TPU v7x, 128 devices: a whole 4x4x4 slice. The times are simulated.
128 devices in a mesh: src: 16 (over z_hi, x, core), snode: 8 (over y, z_lo).
Axes of the slice: x: 4, y: 4, z: 4 (z_hi: 2, z_lo: 2; z = z_hi * 2 + z_lo), core: 2. Of those that a mesh axis runs over, the one named last changes fastest.
Arguments:
- leaf_rhs: float32 [64, 256, 2048], P('snode', None, 'src'), may hold values from -6 to 6
- top_rhs: float32 [2048, 2048], P(None, 'src'), may hold values from -6 to 6
- leaf_inv: float32 [64, 256, 256], P('snode'), may hold values from -1 to 1, as said below
- coupling: float32 [64, 2048, 256], P('snode'), may hold values from -0.046875 to 0.046875
- top_inv: float32 [2048, 2048], P('snode'), may hold values from -1 to 1, as said below
- cond: float32 [64, 256], P('snode'), may hold values from 0.1 to 3
- electrodes: int32 [8192, 4], P('src'), may hold values from 0 to 2047, all different within a row
- blocks: int32 [16, 8192], P(None, 'src'), may hold values from 0 to 63
Outputs:
- sens: float32 [16, 256, 8192], P('snode', None, 'src')
Inputs may be any that keep to these rules, and one draw needn't show every extreme that they name: `electrodes`: the four sources of a row are different. `leaf_inv`: zero above the diagonal of each block. `top_inv`: zero above the diagonal.
All inputs are finite; a program needn't handle non-finite values.
Results may differ from a plain program's by a relative error of at most 0.00011.
Values sent between devices are 32-bit elements; how exact they have to be, the bound alone decides.
No kernel may reach another device: no remote copies, remote signals or barrier semaphores. Data moves between devices by JAX's collectives and lax.ppermute only.
A program may use at most 320 MiB of HBM per device.

v0:
```python
import jax
import jax.numpy as jnp
from jax import lax
from jax.sharding import PartitionSpec as P


def local(leaf_rhs, top_rhs, leaf_inv, coupling, top_inv, cond, electrodes, blocks):
    highest = lax.Precision.HIGHEST
    forward_leaf = jnp.einsum("bij,bjs->bis", leaf_inv, leaf_rhs, precision=highest)
    partial_value = jnp.einsum("bti,bis->ts", coupling, forward_leaf, precision=highest)
    coupled = lax.psum(partial_value, "snode")
    residual = top_rhs - coupled
    forward_top = jnp.dot(top_inv, residual, precision=highest)
    top_partial = jnp.einsum("rt,rs->ts", top_inv, forward_top, precision=highest)
    separator_field = lax.psum(top_partial, "snode")
    adjusted = forward_leaf - jnp.einsum(
        "bti,ts->bis", coupling, separator_field, precision=highest
    )
    leaf_field = jnp.einsum("bji,bjs->bis", leaf_inv, adjusted, precision=highest)
    leaves = leaf_field.shape[0]
    cells_n = leaf_field.shape[1]
    quads_n = electrodes.shape[0]
    shard_piece = lax.all_gather(leaf_field, "src", axis=2, tiled=True)
    width_n = shard_piece.shape[2]
    source_ids = lax.broadcasted_iota(jnp.int32, (width_n, quads_n), 0)

    def signed(plus_ids, minus_ids):
        upper = (source_ids == plus_ids[None, :]).astype(jnp.float32)
        lower = (source_ids == minus_ids[None, :]).astype(jnp.float32)
        return upper - lower

    current_sel = signed(electrodes[:, 0], electrodes[:, 1])
    potential_sel = signed(electrodes[:, 2], electrodes[:, 3])
    current_add = jnp.einsum("bcs,sq->bcq", shard_piece, current_sel, precision=highest)
    potential_add = jnp.einsum("bcs,sq->bcq", shard_piece, potential_sel, precision=highest)
    product = current_add * potential_add
    weighted = cond[:, :, None] * product
    owner_id = lax.axis_index("snode")
    local_blocks = blocks - owner_id * leaves
    own_rows = blocks.shape[0] // lax.axis_size("snode")
    summed = jnp.zeros((own_rows * lax.axis_size("snode"), cells_n, quads_n), jnp.float32)
    for leaf_id in range(leaves):
        summed = summed + jnp.where(
            (local_blocks == leaf_id)[:, None, :], weighted[leaf_id][None], 0.0
        )
    return lax.psum_scatter(summed, "snode", scatter_dimension=0, tiled=True)


def solution(mesh):
    return jax.shard_map(
        local,
        mesh=mesh,
        in_specs=(
            P("snode", None, "src"),
            P(None, "src"),
            P("snode", None, None),
            P("snode", None, None),
            P("snode", None),
            P("snode", None),
            P("src", None),
            P(None, "src"),
        ),
        out_specs=P("snode", None, "src"),
        check_vma=False,
    )
```

profile of v0, /device:TPU:0, one launch (start us, length us, event | category | flops | bytes accessed | tf_op | source)
XLA Modules:
  0.0 582.1 jit_solution(11139085248551137085)
XLA Ops:
  6.5 0.0 copy-start
  6.5 0.0 all-reduce.3.cloned.1.call-start
  6.5 1.6 copy-done
  8.1 3.2 fusion.21
  11.3 17.2 %convolution_bitcast_fusion = f32[2048,128]{1,0:T(8,128)} fusion(f32[8,256,128]{2,1,0:T(8,128)S(1)} %fusion.21, f32[8,2048,256]{2,1,0:T(8,128)} %param.11), kind=kOutput, calls=%fused_computation.16 | convolution fusion | flops 6442450944 | bytes 18874368 | tf_op jit(solution)/shard_map/bti,bis->ts/dot_general | solution.py:10
  28.6 0.0 all-reduce.3.cloned.1.call-update
  28.6 0.0 all-reduce.5.cloned.1.call-start
  28.6 80.3 %all-reduce.3.cloned.1.call-done = f32[2048,128]{1,0:T(8,128)} async-done(((f32[2048,128]{1,0:T(8,128)}), f32[2048,128]{1,0:T(8,128)}) %all-reduce.3.cloned.1.call-update) | async-done | bytes 1048592 | tf_op jit(solution)/shard_map/psum | solution.py:11
  109.0 4.2 fusion.18
  113.2 0.0 copy-done.2
  113.2 2.2 convolution_bitcast_fusion.1
  115.4 0.0 all-reduce.5.cloned.1.call-update
  115.4 0.3 all-gather.2.cloned.1.call-start
  115.8 77.3 %all-reduce.5.cloned.1.call-done = f32[2048,128]{0,1:T(8,128)} async-done(((f32[2048,128]{0,1:T(8,128)}), f32[2048,128]{0,1:T(8,128)}) %all-reduce.5.cloned.1.call-update) | async-done | bytes 1048592 | tf_op jit(solution)/shard_map/psum | solution.py:15
  193.0 29.2 %fusion.16 = f32[8,256,128]{2,1,0:T(8,128)S(1)} fusion(f32[8,256,128]{2,1,0:T(8,128)S(1)} %fusion.21, f32[8,2048,256]{2,1,0:T(8,128)} %param.11, f32[2048,128]{0,1:T(8,128)} %all-reduce.5.cloned.1.call-done), kind=kOutput, calls=%fused_computation.24 | convolution fusion | flops 6442713088 | bytes 19922944 | tf_op jit(solution)/shard_map/bti,ts->bis/dot_general | solution.py:16
  222.2 0.0 copy-start.4
  222.3 0.0 copy-start.3
  222.3 3.0 convolution_bitcast_fusion.2
  225.3 0.0 all-gather.2.cloned.1.call-update
  225.3 0.6 reduce-scatter.2.cloned.1.call-start
  225.9 0.0 copy-done.4
  225.9 0.0 copy-done.3
  226.0 109.3 %all-gather.2.cloned.1.call-done = f32[8,256,2048]{1,2,0:T(8,128)} async-done(((f32[8,256,128]{1,2,0:T(8,128)}), f32[8,256,2048]{1,2,0:T(8,128)}) %all-gather.2.cloned.1.call-update) | async-done | bytes 16777232 | tf_op jit(solution)/shard_map/all_gather | solution.py:23
  335.3 32.1 %fusion = f32[8,256,512]{2,1,0:T(8,128)S(1)} fusion(f32[8,256,2048]{1,2,0:T(8,128)} %all-gather.2.cloned.1.call-done, s32[512]{0:T(512)S(1)} %bitcast.57, s32[512]{0:T(512)S(1)} %bitcast.58), kind=kOutput, calls=%fused_computation.1 | convolution fusion | flops 25775046656 | bytes 20975616 | tf_op jit(solution)/shard_map/bcs,sq->bcq/dot_general | solution.py:35
  367.4 0.0 copy-done.5
  367.4 0.0 copy-done.6
  367.4 30.3 %multiply_multiply_fusion = f32[8,256,512]{2,1,0:T(8,128)S(1)} fusion(f32[8,256,512]{2,1,0:T(8,128)S(1)} %fusion, f32[8,256,2048]{1,2,0:T(8,128)S(1)} %copy-done.5, s32[512]{0:T(512)S(1)} %bitcast.56, s32[512]{0:T(512)S(1)} %bitcast.55, f32[8,256]{1,0:T(8,128)S(1)} %copy-done.6), kind=kOutput, calls=%fused_computation.5 | convolution fusion | flops 25777143808 | bytes 25178112 | tf_op jit(solution)/shard_map/bcs,sq->bcq/dot_general | solution.py:34
  397.7 0.5 slice_bitcast_fusion.7
  398.2 10.2 %select_add_fusion = f32[16,256,512]{2,1,0:T(8,128)} fusion(f32[256,512]{1,0:T(8,128)S(1)} %get-tuple-element.6, f32[256,512]{1,0:T(8,128)S(1)} %get-tuple-element.7, f32[256,512]{1,0:T(8,128)S(1)} %get-tuple-element.8, f32[256,512]{1,0:T(8,128)S(1)} %get-tuple-element.9, f32[256,512]{1,0:T(8,128)S(1)} %get-tuple-element.10, ...), kind=kLoop, calls=%fused_computation | loop fusion | flops 31457280 | bytes 12648448 | tf_op jit(solution)/shard_map/add | solution.py:43
  408.3 0.0 reduce-scatter.2.cloned.1.call-update
  408.4 167.0 %reduce-scatter.2.cloned.1.call-done = f32[2,256,512]{2,1,0:T(8,128)} async-done(((f32[16,256,512]{2,1,0:T(8,128)}), f32[2,256,512]{2,1,0:T(8,128)}) %reduce-scatter.2.cloned.1.call-update) | async-done | bytes 1048592 | tf_op jit(solution)/shard_map/reduce_scatter | solution.py:46
  575.3 0.0 copy-done.1
  (6 shorter events, 0.1 us)
Async XLA Ops:
  6.5 1.6 copy-start
  6.5 102.4 %all-reduce.3.cloned.1.call-start = ((), (), s32[]{:S(2)}) async-start(), calls=%async_computation.1 | async-start | bytes 2097152 | tf_op jit(solution)/shard_map/psum | solution.py:11
  28.6 164.5 %all-reduce.5.cloned.1.call-start = ((), (), s32[]{:S(2)}) async-start(), calls=%async_computation.2 | async-start | bytes 2097152 | tf_op jit(solution)/shard_map/psum | solution.py:15
  109.0 4.2 copy-start.2
  115.4 219.9 %all-gather.2.cloned.1.call-start = ((), (), s32[]{:S(2)}) async-start(), calls=%async_computation.3 | async-start | bytes 17825792 | tf_op jit(solution)/shard_map/all_gather | solution.py:23
  222.2 3.6 copy-start.4
  222.3 3.6 copy-start.3
  225.3 350.0 %reduce-scatter.2.cloned.1.call-start = ((), (), s32[]{:S(2)}) async-start(), calls=%async_computation.4 | async-start | bytes 9437184 | tf_op jit(solution)/shard_map/reduce_scatter | solution.py:46
  335.3 32.1 %copy-start.5 = (f32[8,256,2048]{1,2,0:T(8,128)S(1)}, f32[8,256,2048]{1,2,0:T(8,128)}, u32[]{:S(2)}) copy-start(f32[8,256,2048]{1,2,0:T(8,128)} %all-gather.2.cloned.1.call-done) | copy-start | bytes 50331652
  335.3 32.1 %copy-start.6 = (f32[8,256]{1,0:T(8,128)S(1)}, f32[8,256]{1,0:T(8,128)}, u32[]{:S(2)}) copy-start(f32[8,256]{1,0:T(8,128)} %param.13) | copy-start | bytes 24580
  408.3 167.0 %copy-start.1 = (f32[8,256,256]{2,1,0:T(8,128)S(1)}, f32[8,256,256]{2,1,0:T(8,128)}, u32[]{:S(2)}) copy-start(f32[8,256,256]{2,1,0:T(8,128)} %param.10) | copy-start | bytes 6291460
Sparse Core Ops, SparseCore 0:
  28.7 80.1 all-reduce.2
  115.5 77.4 all-reduce.4
  225.4 109.8 all-gather.1
  408.5 166.7 reduce-scatter.1
where the time goes:
time: 590 us; the launch traced here: 582 us
  waiting for transfers between devices  434 us (74%)
  matrix products  121 us (21%)
  between operations  13.5 us (2%)
  other arithmetic  10.2 us (2%)
    reduce_scatter x1, waiting for transfers between devices, local(): return lax.psum_scatter(summed, 'snode', scatter_dimension=0, tiled=True)  167 us
    all_gather x1, waiting for transfers between devices, local(): shard_piece = lax.all_gather(leaf_field, 'src', axis=2, tiled=True)  109 us
    psum x1, waiting for transfers between devices, local(): coupled = lax.psum(partial_value, 'snode')  80.3 us
    psum x1, waiting for transfers between devices, local(): separator_field = lax.psum(top_partial, 'snode')  77.3 us
    dot_general x1, matrix products, local(): jnp.einsum('bcs,sq->bcq', shard_piece, potential_sel, precision=highest)  32.1 us
    dot_general x1, matrix products, local(): jnp.einsum('bcs,sq->bcq', shard_piece, current_sel, precision=highest)  30.3 us
    dot_general x1, matrix products, local(): jnp.einsum('bti,ts->bis', coupling, separator_field, precision=highest)  29.2 us
    dot_general x1, matrix products, local(): jnp.einsum('bti,bis->ts', coupling, forward_leaf, precision=highest)  17.2 us
  transfers between devices with their start and end apart: 4, of which 4 were waited for; matrix products, arithmetic and copies ran while one was open for 0% of the time, Pallas kernels for 0%

commit v1 on v0

v1 whole, which is shorter than its diff:
```python
import jax
import jax.numpy as jnp
import numpy as np
from jax import lax
from jax.experimental import pallas as pl
from jax.experimental.pallas import tpu as pltpu
from jax.sharding import Mesh, PartitionSpec as P

HIGH = lax.Precision.HIGH
HIGHEST = lax.Precision.HIGHEST
UNROLL = 32
CHIPS = 64


def leaf_kernel(inv_ref, adjusted_ref, cond_ref, out_ref):
    for j in range(8):
        field = lax.dot_general(
            inv_ref[j], adjusted_ref[j], (((0,), (0,)), ((), ())),
            precision=HIGHEST, preferred_element_type=jnp.float32,
        )
        weight = jnp.sqrt(cond_ref[j : j + 1, :])
        field = field * jnp.broadcast_to(weight, (128, 256)).T
        for c4 in range(4):
            row = (c4 // 2) * 16 + j * 2 + c4 % 2
            out_ref[pl.ds(row, CHIPS, stride=32), :] = field[c4 * CHIPS : (c4 + 1) * CHIPS, :]


def leaf_send(inv, adjusted, cond):
    return pl.pallas_call(
        leaf_kernel,
        out_shape=jax.ShapeDtypeStruct((CHIPS * 32, 128), jnp.float32),
        compiler_params=pltpu.CompilerParams(vmem_limit_bytes=32 << 20),
        name="leaf_send",
    )(inv, adjusted, cond)


def select_kernel(el_ref, bl_ref, even_ref, odd_ref, out_ref, rows_ref, prod_ref):
    @pl.when(pl.program_id(0) == 0)
    def _():
        for chip in range(8):
            for core, ref in enumerate((even_ref, odd_ref)):
                for half in range(2):
                    parts = [ref[chip, p * 32 + half * 16 : p * 32 + half * 16 + 16, :] for p in range(8)]
                    at = (chip * 2 + core) * 128
                    rows_ref[at : at + 128, half, :] = jnp.concatenate(parts, axis=0).T

    quads_n = prod_ref.shape[0] // 2

    def body(group, carry):
        base = pl.multiple_of(group * UNROLL, UNROLL)
        for step in range(UNROLL):
            q = base + step
            a = rows_ref[el_ref[q]]
            b = rows_ref[el_ref[quads_n + q]]
            c = rows_ref[el_ref[2 * quads_n + q]]
            d = rows_ref[el_ref[3 * quads_n + q]]
            prod_ref[pl.ds(2 * base + 2 * step, 2), :] = (a - b) * (c - d)
        return carry

    lax.fori_loop(0, quads_n // UNROLL, body, 0)
    for t in range(quads_n // 128):
        lanes = bl_ref[0, :, t * 128 : (t + 1) * 128] * 2
        ids = jnp.concatenate([lanes, lanes + 1, jnp.zeros((96, 128), jnp.int32)], axis=0).T
        for half in range(2):
            prod = prod_ref[pl.ds(t * 256 + half, 128, stride=2), :]
            sel = jnp.take_along_axis(prod, ids, axis=1).T
            for p in range(8):
                for c2 in range(2):
                    at = c2 * 16 + 2 * p
                    to = t * 8 + (half * 2 + c2) * 2
                    out_ref[p, to : to + 2, :] = sel[at : at + 2, :]


def select(el, bl, even, odd):
    return pl.pallas_call(
        select_kernel,
        grid=(8,),
        out_shape=jax.ShapeDtypeStruct((CHIPS, 32, 128), jnp.float32),
        in_specs=[
            pl.BlockSpec((2048,), lambda i: (i,), memory_space=pltpu.SMEM),
            pl.BlockSpec((1, 16, 512), lambda i: (i, 0, 0)),
            pl.BlockSpec((8, 256, 128), lambda i: (0, 0, 0)),
            pl.BlockSpec((8, 256, 128), lambda i: (0, 0, 0)),
        ],
        out_specs=pl.BlockSpec((8, 32, 128), lambda i: (i, 0, 0)),
        scratch_shapes=[
            pltpu.VMEM((2048, 2, 128), jnp.float32),
            pltpu.VMEM((1024, 128), jnp.float32),
        ],
        compiler_params=pltpu.CompilerParams(vmem_limit_bytes=32 << 20),
        name="select_quads",
    )(el, bl, even, odd)


def assemble_kernel(in_ref, out_ref):
    for t in range(4):
        for c4 in range(4):
            for k2 in range(2):
                out_ref[k2, c4 * CHIPS : (c4 + 1) * CHIPS, t * 128 : (t + 1) * 128] = in_ref[
                    pl.ds(t * 8 + c4 * 2 + k2, CHIPS, stride=32), :
                ]


def assemble(received):
    return pl.pallas_call(
        assemble_kernel,
        out_shape=jax.ShapeDtypeStruct((2, 256, 512), jnp.float32),
        name="assemble_sens",
    )(received)


def reduce_scatter(value, rows):
    parts = lax.all_to_all(value.reshape(8, rows, -1), "snode", 0, 0, tiled=True)
    return jnp.sum(parts, axis=0)


def all_gather(block):
    whole = jnp.broadcast_to(block[None], (8,) + block.shape)
    return lax.all_to_all(whole, "snode", 0, 0, tiled=True).reshape(8 * block.shape[0], -1)


def local(leaf_rhs, top_rhs, leaf_inv, coupling, top_inv, cond, electrodes, blocks):
    me = lax.axis_index("snode")

    lists = jnp.concatenate([electrodes.T, blocks, jnp.zeros((12, 512), jnp.int32)], axis=0)
    lists = lax.all_gather(lists.astype(jnp.float32).reshape(128, 128), ("chip", "core"), axis=0, tiled=True)
    lists = lists.reshape(8, 2, 32, 512)
    lists = lax.dynamic_index_in_dim(lists, lax.axis_index("core"), 1, keepdims=False).astype(jnp.int32)
    el = lists[:, :4].reshape(8 * 2048)
    bl = lists[:, 4:20]

    forward_leaf = jnp.einsum("bij,bjs->bis", leaf_inv, leaf_rhs, precision=HIGH)
    partial_value = jnp.einsum("bti,bis->ts", coupling, forward_leaf, precision=HIGH)
    coupled = reduce_scatter(partial_value, 256)
    residual = lax.dynamic_slice_in_dim(top_rhs, me * 256, 256, 0) - coupled
    residual = all_gather(residual)
    forward_top = jnp.dot(top_inv, residual, precision=HIGH)
    top_partial = jnp.einsum("rt,rs->ts", top_inv, forward_top, precision=HIGH)
    separator_field = all_gather(reduce_scatter(top_partial, 256))
    adjusted = forward_leaf - jnp.einsum("bti,ts->bis", coupling, separator_field, precision=HIGH)

    send = leaf_send(leaf_inv, adjusted, cond)
    own = lax.all_to_all(send.reshape(CHIPS, 32, 128), ("chip", "snode"), 0, 0, tiled=True)
    own = own.reshape(8, 256, 128)
    other = lax.ppermute(own, "core", [(0, 1), (1, 0)])
    odd = lax.axis_index("core") == 1
    picked = select(el, bl, jnp.where(odd, other, own), jnp.where(odd, own, other))
    received = lax.all_to_all(picked, ("chip", "snode"), 0, 0, tiled=True)
    return assemble(received.reshape(CHIPS * 32, 128))


def solution(mesh):
    devices = np.asarray(mesh.devices)
    fine = Mesh(devices.reshape(8, 2, 8), ("chip", "core", "snode"))
    src = ("chip", "core")
    return jax.shard_map(
        local,
        mesh=fine,
        in_specs=(
            P("snode", None, src),
            P(None, src),
            P("snode", None, None),
            P("snode", None, None),
            P("snode", None),
            P("snode", None),
            P(src, None),
            P(None, src),
        ),
        out_specs=P("snode", None, src),
        check_vma=False,
    )
```

time: 590 us -> 217 us (0.37); the launches traced: 582 us -> 216 us
  waiting for transfers between devices: 434 us -> 26.2 us
  matrix products: 121 us -> 34 us
  blocking collectives: 0 us -> 83.3 us
  Pallas kernels: 0 us -> 31.8 us
  local copies, waits for them, and re-layouts: 2.08 us -> 11.7 us
  starting transfers between devices: 0.94 us -> 10.4 us
    reduce_scatter x1 -> x0, waiting for transfers between devices: 167 us -> none  [local(): return lax.psum_scatter(summed, 'snode', scatter_dimension=0, tiled=True)]
    psum x2 -> x0, waiting for transfers between devices: 158 us -> none  [the longest x1 80.3 us: local(): coupled = lax.psum(partial_value, 'snode')]
    all_gather x1, waiting for transfers between devices: 109 us -> 0.01 us  [local(): lax.all_gather(lists.astype(jnp.float32).reshape(128, 128), ('chip', 'cor...]
    dot_general x8 -> x5, matrix products: 121 us -> 34 us  [the longest x1 17.1 us: local(): jnp.einsum('bti,ts->bis', coupling, separator_field, precision=HIGH)]
    all_to_all x0 -> x4, blocking collectives: none -> 83.3 us  [the longest x1 25.1 us: local(): lax.all_to_all(send.reshape(CHIPS, 32, 128), ('chip', 'snode'), 0, 0, til...]
    pallas_call x0 -> x3, Pallas kernels: none -> 31.8 us  [the longest x1 26.4 us: select(): pl.pallas_call(select_kernel, grid=(8,), out_shape=jax.ShapeDtypeStruct((...]
    all_to_all x0 -> x2, waiting for transfers between devices: none -> 26.2 us  [the longest x1 14.9 us: reduce_scatter(): lax.all_to_all(value.reshape(8, rows, -1), 'snode', 0, 0, tiled=True)]
    add x1 -> x0, other arithmetic: 10.2 us -> none  [local(): summed + jnp.where((local_blocks == leaf_id)[:, None, :], weighted[leaf_i...]
  transfers between devices with their start and end apart: 4 -> 4, of which waited for: 4 -> 2; matrix products, arithmetic and copies ran while one was open for 0% -> 13% of each run, Pallas kernels for 0% -> 1%
where the time goes in v1:
time: 217 us; the launch traced here: 216 us
  blocking collectives  83.3 us (38%)
  matrix products  34 us (16%)
  Pallas kernels  31.8 us (15%)
  waiting for transfers between devices  26.2 us (12%)
  between operations  13.6 us (6%)
  local copies, waits for them, and re-layouts  11.7 us (5%)
  starting transfers between devices  10.4 us (5%)
  other arithmetic  5.24 us (2%)
    pallas_call x1, Pallas kernels, select(): pl.pallas_call(select_kernel, grid=(8,), out_shape=jax.ShapeDtypeStruct((...  26.4 us
    all_to_all x1, blocking collectives, local(): lax.all_to_all(send.reshape(CHIPS, 32, 128), ('chip', 'snode'), 0, 0, til...  25.1 us
    all_to_all x1, blocking collectives, local(): received = lax.all_to_all(picked, ('chip', 'snode'), 0, 0, tiled=True)  24.2 us
    all_to_all x1, blocking collectives, all_gather(): lax.all_to_all(whole, 'snode', 0, 0, tiled=True)  17.3 us
    dot_general x1, matrix products, local(): jnp.einsum('bti,ts->bis', coupling, separator_field, precision=HIGH)  17.1 us
    all_to_all x1, blocking collectives, reduce_scatter(): lax.all_to_all(value.reshape(8, rows, -1), 'snode', 0, 0, tiled=True)  16.7 us
    all_to_all x1, waiting for transfers between devices, reduce_scatter(): lax.all_to_all(value.reshape(8, rows, -1), 'snode', 0, 0, tiled=True)  14.9 us
    dot_general x1, matrix products, local(): jnp.einsum('bti,bis->ts', coupling, forward_leaf, precision=HIGH)  12.1 us
  transfers between devices with their start and end apart: 4, of which 2 were waited for; matrix products, arithmetic and copies ran while one was open for 13% of the time, Pallas kernels for 1%

profile of v1, /device:TPU:0, one launch (start us, length us, event | category | flops | bytes accessed | tf_op | source)
XLA Modules:
  0.0 216.3 jit_solution(15291563986469191490)
XLA Ops:
  6.5 3.0 %fusion.2 = f32[8,256,128]{2,1,0:T(8,128)S(1)} fusion(f32[8,256,256]{2,1,0:T(8,128)} %inv_ref.1, f32[8,256,128]{2,1,0:T(8,128)} %param.8), kind=kOutput, calls=%fused_computation.11 | convolution fusion | flops 402653184 | bytes 4194304 | tf_op jit(solution)/shard_map/bij,bjs->bis/dot_general | solution.py:132
  9.5 12.1 %fusion.3 = f32[128,2048,1]{1,0,2:T(8,128)S(1)} fusion(f32[8,256,128]{2,1,0:T(8,128)S(1)} %fusion.2, f32[8,2048,256]{2,1,0:T(8,128)} %param.11), kind=kOutput, calls=%fused_computation.12 | convolution fusion | flops 3221225472 | bytes 18874368 | tf_op jit(solution)/shard_map/bti,bis->ts/dot_general | solution.py:133
  21.7 1.1 copy.34
  22.7 5.9 %all-to-all-start = ((f32[8,256,128]{1,2,0:T(8,128)}), f32[8,256,128]{1,2,0:T(8,128)}, u32[]{:S(2)}, u32[]{:S(2)}) async-start(f32[8,256,128]{1,2,0:T(8,128)} %bitcast.52), calls=%async_computation | async-start | bytes 2097152 | tf_op jit(solution)/shard_map/all_to_all | solution.py:113
  28.7 0.9 constant_dynamic-slice_fusion
  29.6 0.1 copy.27
  29.7 14.9 %all-to-all-done = f32[8,256,128]{1,2,0:T(8,128)} async-done(((f32[8,256,128]{1,2,0:T(8,128)}), f32[8,256,128]{1,2,0:T(8,128)}, u32[]{:S(2)}, u32[]{:S(2)}) %all-to-all-start) | async-done | bytes 1048608 | tf_op jit(solution)/shard_map/all_to_all | solution.py:113
  44.6 1.3 reduce_sum.18
  45.9 0.1 copy.19
  46.1 17.3 %all_to_all.30 = f32[8,256,128]{2,1,0:T(8,128)S(1)} all-to-all(f32[8,256,128]{2,1,0:T(8,128)S(1)} %broadcast_in_dim.7), channel_id=1, replica_groups=mesh['chip'=8,'core'=2,'snode'=8] {'snode'}, dimensions={0} | all-to-all | bytes 2097152 | tf_op jit(solution)/shard_map/all_to_all | solution.py:119
  63.4 1.0 fusion.4
  64.5 0.7 fusion.5
  65.2 0.1 copy.33
  65.3 16.7 %all_to_all.31 = f32[8,256,128]{1,2,0:T(8,128)} all-to-all(f32[8,256,128]{1,2,0:T(8,128)S(1)} %bitcast.53), channel_id=1, replica_groups=mesh['chip'=8,'core'=2,'snode'=8] {'snode'}, dimensions={0} | all-to-all | bytes 2097152 | tf_op jit(solution)/shard_map/all_to_all | solution.py:113
  82.0 1.3 reduce_sum.19
  83.4 1.1 broadcast_in_dim.8
  84.4 4.3 %all-to-all-start.3 = ((f32[8,256,128]{1,2,0:T(8,128)}), f32[8,256,128]{1,2,0:T(8,128)}, u32[]{:S(2)}, u32[]{:S(2)}) async-start(f32[8,256,128]{1,2,0:T(8,128)} %broadcast_in_dim.8), calls=%async_computation.3 | async-start | bytes 2097152 | tf_op jit(solution)/shard_map/all_to_all | solution.py:119
  88.7 0.2 all-gather.2.cloned.1.call-start
  89.0 0.1 add_convert_fusion
  89.1 0.6 convert_element_type.14
  89.7 11.3 %all-to-all-done.3 = f32[8,256,128]{1,2,0:T(8,128)} async-done(((f32[8,256,128]{1,2,0:T(8,128)}), f32[8,256,128]{1,2,0:T(8,128)}, u32[]{:S(2)}, u32[]{:S(2)}) %all-to-all-start.3) | async-done | bytes 1048608 | tf_op jit(solution)/shard_map/all_to_all | solution.py:119
  101.0 2.8 %copy.21 = f32[8,256,128]{1,0,2:T(8,128)} copy(f32[8,256,128]{1,2,0:T(8,128)} %all-to-all-done.3) | data formatting | bytes 2097152 | tf_op jit(solution)/shard_map/all_to_all | solution.py:119
  103.8 2.4 %reshape.43 = f32[2048,128,1]{0,1,2:T(8,128)} reshape(f32[8,256,128]{1,0,2:T(8,128)} %copy.21) | data formatting | bytes 2097152 | tf_op jit(solution)/shard_map/reshape | solution.py:119
  106.2 17.1 %fusion.adjusted_ref = f32[8,256,128]{2,1,0:T(8,128)S(1)} fusion(f32[8,256,128]{2,1,0:T(8,128)S(1)} %fusion.2, f32[2048,128,1]{0,1,2:T(8,128)} %reshape.43, f32[8,2048,256]{2,1,0:T(8,128)} %param.11), kind=kOutput, calls=%fused_computation.1 | convolution fusion | flops 3221487616 | bytes 19922944 | tf_op jit(solution)/shard_map/bti,ts->bis/dot_general | solution.py:140
  123.4 2.6 %leaf_send.1 = f32[2048,128]{1,0:T(8,128)S(1)} custom-call(f32[8,256,256]{2,1,0:T(8,128)S(1)} %copy-done.1, f32[8,256,128]{2,1,0:T(8,128)S(1)} %fusion.adjusted_ref, f32[8,256]{1,0:T(8,128)S(1)} %copy-done.2), custom_call_target="tpu_custom_call" | custom-call | tf_op jit(solution)/shard_map/leaf_send/pallas_call | solution.py:29
  126.0 25.1 %all_to_all.32 = f32[64,32,128]{2,1,0:T(8,128)S(1)} all-to-all(f32[64,32,128]{2,1,0:T(8,128)S(1)} %bitcast.45), channel_id=1, replica_groups=mesh['chip'=8,'core'=2,'snode'=8] {'chip','snode'}, dimensions={0} | all-to-all | bytes 2097152 | tf_op jit(solution)/shard_map/all_to_all | solution.py:143
  151.1 2.4 %reshape.33 = f32[8,2,32,512]{3,2,1,0:T(8,128)} reshape(f32[2048,128]{1,0:T(8,128)} %all-gather.2.cloned.1.call-done) | data formatting | bytes 2097152 | tf_op jit(solution)/shard_map/reshape | solution.py:127
  153.4 1.1 fusion.1
  154.6 1.4 broadcast_select_fusion
  156.1 26.4 %select_quads.1 = f32[64,32,128]{2,1,0:T(8,128)S(1)} custom-call(s32[16384]{0:T(1024)S(1)} %bitcast.46, s32[8,16,512]{2,1,0:T(8,128)S(1)} %slice.9.bl_ref, f32[8,256,128]{2,1,0:T(8,128)S(1)} %get-tuple-element.6.even_ref, f32[8,256,128]{2,1,0:T(8,128)S(1)} %get-tuple-element.5.odd_ref), custom_call_target="tpu_custom_call" | custom-call | tf_op jit(solution)/shard_map/select_quads/pallas_call | solution.py:75
  182.4 24.2 %all_to_all.33 = f32[64,32,128]{2,1,0:T(8,128)} all-to-all(f32[64,32,128]{2,1,0:T(8,128)S(1)} %select_quads.1), channel_id=1, replica_groups=mesh['chip'=8,'core'=2,'snode'=8] {'chip','snode'}, dimensions={0} | all-to-all | bytes 2097152 | tf_op jit(solution)/shard_map/all_to_all | solution.py:148
  206.6 2.8 %assemble_sens.1 = f32[2,256,512]{2,1,0:T(8,128)} custom-call(f32[2048,128]{1,0:T(8,128)} %bitcast.54), custom_call_target="tpu_custom_call" | custom-call | tf_op jit(solution)/shard_map/assemble_sens/pallas_call | solution.py:105
  (21 shorter events, 0.3 us)
Async XLA Ops:
  6.5 56.9 %copy-start = (f32[256,2048]{1,0:T(8,128)S(1)}, f32[256,2048]{1,0:T(8,128)}, u32[]{:S(2)}) copy-start(f32[256,2048]{1,0:T(8,128)} %param.12) | copy-start | bytes 6291460
  22.7 21.9 %all-to-all-start = ((f32[8,256,128]{1,2,0:T(8,128)}), f32[8,256,128]{1,2,0:T(8,128)}, u32[]{:S(2)}, u32[]{:S(2)}) async-start(f32[8,256,128]{1,2,0:T(8,128)} %bitcast.52), calls=%async_computation | async-start | bytes 2097152 | tf_op jit(solution)/shard_map/all_to_all | solution.py:113
  82.0 7.0 %copy-start.3 = (s32[16,512]{1,0:T(8,128)S(1)}, s32[16,512]{1,0:T(8,128)}, u32[]{:S(2)}) copy-start(s32[16,512]{1,0:T(8,128)} %param.15) | copy-start | bytes 98308
  82.0 7.0 %copy-start.4 = (s32[512,4]{0,1:T(4,128)S(1)}, s32[512,4]{0,1:T(4,128)}, u32[]{:S(2)}) copy-start(s32[512,4]{0,1:T(4,128)} %param.14) | copy-start | bytes 24580
  84.4 16.6 %all-to-all-start.3 = ((f32[8,256,128]{1,2,0:T(8,128)}), f32[8,256,128]{1,2,0:T(8,128)}, u32[]{:S(2)}, u32[]{:S(2)}) async-start(f32[8,256,128]{1,2,0:T(8,128)} %broadcast_in_dim.8), calls=%async_computation.3 | async-start | bytes 2097152 | tf_op jit(solution)/shard_map/all_to_all | solution.py:119
  88.7 62.4 %all-gather.2.cloned.1.call-start = ((), (), s32[]{:S(2)}) async-start(), calls=%async_computation.6 | async-start | bytes 1114112 | tf_op jit(solution)/shard_map/all_gather | solution.py:126
  106.2 17.1 %copy-start.1 = (f32[8,256,256]{2,1,0:T(8,128)S(1)}, f32[8,256,256]{2,1,0:T(8,128)}, u32[]{:S(2)}) copy-start(f32[8,256,256]{2,1,0:T(8,128)} %inv_ref.1) | copy-start | bytes 6291460
  106.2 17.1 %copy-start.2 = (f32[8,256]{1,0:T(8,128)S(1)}, f32[8,256]{1,0:T(8,128)}, u32[]{:S(2)}) copy-start(f32[8,256]{1,0:T(8,128)} %cond_ref.1) | copy-start | bytes 24580
  151.1 3.5 %collective-permute-start = (f32[8,256,128]{2,1,0:T(8,128)S(1)}, f32[8,256,128]{2,1,0:T(8,128)}, u32[]{:S(2)}, u32[]{:S(2)}) collective-permute-start(f32[8,256,128]{2,1,0:T(8,128)S(1)} %bitcast.47), channel_id=1, source_target_pairs={{0,8},{8,0},{1,9},{9,1},{2,10},{10,2},{3,11},{11,3},{4,12},{12,4},... | collective-permute-start | bytes 3145736 | tf_op jit(solution)/shard_map/ppermute | solution.py:145
Sparse Core Ops, SparseCore 0:
  92.0 47.3 all-gather.1

commit v2 on v1

v2 whole, which is shorter than its diff:
```python
import jax
import jax.numpy as jnp
import numpy as np
from jax import lax
from jax.experimental import pallas as pl
from jax.experimental.pallas import tpu as pltpu
from jax.sharding import Mesh, PartitionSpec as P

UNROLL = 64
CHIPS = 64


def two(value):
    high = value.astype(jnp.bfloat16)
    return high, (value - high.astype(jnp.float32)).astype(jnp.bfloat16)


def mm(a, b):
    return jnp.dot(a, b, preferred_element_type=jnp.float32)


def params():
    return pltpu.CompilerParams(vmem_limit_bytes=40 << 20)


def front_kernel(inv_ref, rhs_ref, coupling_ref, sum_ref, forward_ref):
    j = pl.program_id(0)

    @pl.when(j == 0)
    def _():
        sum_ref[...] = jnp.zeros_like(sum_ref)

    ih, il = two(inv_ref[0])
    rh, rl = two(rhs_ref[0])
    both = jnp.concatenate([rh, rl], axis=1)
    wide = mm(ih, both)
    last = mm(il, both)
    forward = wide[:, :128] + (wide[:, 128:] + (last[:, :128] + last[:, 128:]))
    forward_ref[0] = forward.T
    fh, fl = two(forward)
    both = jnp.concatenate([fh, fl], axis=1)
    for r in range(0, coupling_ref.shape[1], 512):
        ch, cl = two(coupling_ref[0, r : r + 512, :])
        wide = mm(ch, both)
        sum_ref[r : r + 512, :] += wide[:, :128] + wide[:, 128:] + mm(cl, fh)


def front(inv, rhs, coupling):
    return pl.pallas_call(
        front_kernel,
        grid=(8,),
        out_shape=(
            jax.ShapeDtypeStruct((2048, 128), jnp.float32),
            jax.ShapeDtypeStruct((8, 128, 256), jnp.float32),
        ),
        in_specs=[
            pl.BlockSpec((1, 256, 256), lambda j: (j, 0, 0)),
            pl.BlockSpec((1, 256, 128), lambda j: (j, 0, 0)),
            pl.BlockSpec((1, 2048, 256), lambda j: (j, 0, 0)),
        ],
        out_specs=(
            pl.BlockSpec((2048, 128), lambda j: (0, 0)),
            pl.BlockSpec((1, 128, 256), lambda j: (j, 0, 0)),
        ),
        compiler_params=params(),
        name="leaf_front",
    )(inv, rhs, coupling)


def residual_kernel(me_ref, parts_ref, top_ref, out_ref):
    value = top_ref[...]
    for p in range(8):
        value = value - parts_ref[p]
    for p in range(8):
        out_ref[p] = value


def residual(me, parts, top):
    return pl.pallas_call(
        residual_kernel,
        grid_spec=pltpu.PrefetchScalarGridSpec(
            num_scalar_prefetch=1,
            grid=(1,),
            in_specs=[
                pl.BlockSpec((8, 256, 128), lambda i, me: (0, 0, 0)),
                pl.BlockSpec((256, 128), lambda i, me: (me[0], 0)),
            ],
            out_specs=pl.BlockSpec((8, 256, 128), lambda i, me: (0, 0, 0)),
        ),
        out_shape=jax.ShapeDtypeStruct((8, 256, 128), jnp.float32),
        compiler_params=params(),
        name="residual",
    )(me, parts, top)


def spread_kernel(parts_ref, out_ref):
    value = parts_ref[0]
    for p in range(1, 8):
        value = value + parts_ref[p]
    for p in range(8):
        out_ref[p] = value


def spread(parts):
    return pl.pallas_call(
        spread_kernel,
        out_shape=jax.ShapeDtypeStruct(parts.shape, jnp.float32),
        compiler_params=params(),
        name="spread",
    )(parts)


def top_kernel(inv_ref, res_ref, out_ref):
    total = None
    for p in range(8):
        th, tl = two(inv_ref[:, p * 256 : (p + 1) * 256])
        rh, rl = two(res_ref[p])
        wide = mm(th, jnp.concatenate([rh, rl], axis=1))
        term = wide[:, :128] + wide[:, 128:] + mm(tl, rh)
        total = term if total is None else total + term
    fh, fl = two(total.T)
    both = jnp.concatenate([fh, fl], axis=0)
    for p in range(8):
        th, tl = two(inv_ref[:, p * 256 : (p + 1) * 256])
        wide = mm(both, th)
        out_ref[p] = wide[:128] + wide[128:] + mm(fh, tl)


def top(inv, res):
    return pl.pallas_call(
        top_kernel,
        out_shape=jax.ShapeDtypeStruct((8, 128, 256), jnp.float32),
        compiler_params=params(),
        name="top_solve",
    )(inv, res)


def back_kernel(sep_ref, forward_ref, coupling_ref, inv_ref, cond_ref, out_ref, split_ref, total_ref):
    j = pl.program_id(0)

    @pl.when(j == 0)
    def _():
        for p in range(8):
            split_ref[p, :128], split_ref[p, 128:] = two(sep_ref[p])

    total = forward_ref[0]
    for p in range(8):
        ch, cl = two(coupling_ref[0, p * 256 : (p + 1) * 256, :])
        wide = mm(split_ref[p], ch)
        total = total - (wide[:128] + wide[128:] + mm(split_ref[p, :128], cl))
    total_ref[j] = total

    @pl.when(j == 7)
    def _():
        for b in range(8):
            th, tl = two(total_ref[b])
            ih, il = two(inv_ref[b])
            both = jnp.concatenate([th, tl], axis=0)
            wide = mm(both, ih)
            last = mm(both, il)
            field = wide[:128] + (wide[128:] + (last[:128] + last[128:]))
            field = (field * jnp.sqrt(cond_ref[b : b + 1, :])).T
            for c4 in range(4):
                row = (c4 // 2) * 16 + b * 2 + c4 % 2
                out_ref[pl.ds(row, CHIPS, stride=32), :] = field[c4 * CHIPS : (c4 + 1) * CHIPS, :]


def back(sep, forward, coupling, inv, cond):
    return pl.pallas_call(
        back_kernel,
        grid=(8,),
        out_shape=jax.ShapeDtypeStruct((CHIPS * 32, 128), jnp.float32),
        in_specs=[
            pl.BlockSpec((8, 128, 256), lambda j: (0, 0, 0)),
            pl.BlockSpec((1, 128, 256), lambda j: (j, 0, 0)),
            pl.BlockSpec((1, 2048, 256), lambda j: (j, 0, 0)),
            pl.BlockSpec((8, 256, 256), lambda j: (0, 0, 0)),
            pl.BlockSpec((8, 256), lambda j: (0, 0)),
        ],
        out_specs=pl.BlockSpec((CHIPS * 32, 128), lambda j: (0, 0)),
        scratch_shapes=[
            pltpu.VMEM((8, 256, 256), jnp.bfloat16),
            pltpu.VMEM((8, 128, 256), jnp.float32),
        ],
        compiler_params=params(),
        name="leaf_back",
    )(sep, forward, coupling, inv, cond)


def select_kernel(core_ref, el_ref, lists_ref, own_ref, other_ref, out_ref, rows_ref, prod_ref, ids_ref):
    @pl.when(pl.program_id(0) == 0)
    def _():
        for chip in range(8):
            for ref, core in ((own_ref, core_ref[0]), (other_ref, 1 - core_ref[0])):
                for half in range(2):
                    parts = [ref[chip, p * 32 + half * 16 : p * 32 + half * 16 + 16, :] for p in range(8)]
                    at = (chip * 2 + core) * 256 + half
                    rows_ref[pl.ds(at, 128, stride=2), :] = jnp.concatenate(parts, axis=0).T

    quads_n = prod_ref.shape[0] // 2

    def field(at):
        return rows_ref[pl.ds(pl.multiple_of(el_ref[at], 2), 2), :]

    def body(group, carry):
        base = pl.multiple_of(group * UNROLL, UNROLL)
        for step in range(UNROLL):
            q = base + step
            a = field(q)
            b = field(quads_n + q)
            c = field(2 * quads_n + q)
            d = field(3 * quads_n + q)
            prod_ref[pl.ds(2 * base + 2 * step, 2), :] = (a - b) * (c - d)
        return carry

    lax.fori_loop(0, quads_n // UNROLL, body, 0)

    lane = lax.broadcasted_iota(jnp.int32, (128, 128), 1)
    second = lane & 8 != 0
    upper = lane & 4 != 0
    for pair in range(2):
        for t2 in range(2):
            for k2 in range(2):
                at = 16 + k2 * 4 + pair * 2 + t2
                lanes = lists_ref[pl.ds(at, 8, stride=8), :].astype(jnp.int32) * 2
                for c2 in range(2):
                    for half in range(2):
                        ids_ref[pl.ds(t2 * 8 + half * 4 + c2 * 2 + k2, 8, stride=16), :] = lanes + c2
        ids = ids_ref[...].T
        tiles = []
        for t2 in range(2):
            for half in range(2):
                prod = prod_ref[pl.ds((pair * 2 + t2) * 256 + half, 128, stride=2), :]
                tiles.append(jnp.take_along_axis(prod, ids, axis=1))
        low = jnp.where(upper, tiles[1], tiles[0])
        high = jnp.where(upper, tiles[3], tiles[2])
        sel = jnp.where(second, high, low).T
        for p in range(8):
            out_ref[p, pair * 16 : (pair + 1) * 16, :] = sel[p * 16 : (p + 1) * 16, :]


def select(core, el, lists, own, other):
    return pl.pallas_call(
        select_kernel,
        grid_spec=pltpu.PrefetchScalarGridSpec(
            num_scalar_prefetch=1,
            grid=(8,),
            in_specs=[
                pl.BlockSpec((2048,), lambda i, core: (i,), memory_space=pltpu.SMEM),
                pl.BlockSpec((128, 128), lambda i, core: (2 * i + core[0], 0)),
                pl.BlockSpec((8, 256, 128), lambda i, core: (0, 0, 0)),
                pl.BlockSpec((8, 256, 128), lambda i, core: (0, 0, 0)),
            ],
            out_specs=pl.BlockSpec((8, 32, 128), lambda i, core: (i, 0, 0)),
            scratch_shapes=[
                pltpu.VMEM((4096, 128), jnp.float32),
                pltpu.VMEM((1024, 128), jnp.float32),
                pltpu.VMEM((128, 128), jnp.int32),
            ],
        ),
        out_shape=jax.ShapeDtypeStruct((CHIPS, 32, 128), jnp.float32),
        compiler_params=params(),
        name="select_quads",
    )(core, el, lists, own, other)


def assemble_kernel(in_ref, out_ref):
    n = out_ref.shape[2]
    for t in range(4):
        for c4 in range(4):
            for k2 in range(2):
                out_ref[k2, c4, :, t * 128 : (t + 1) * 128] = in_ref[
                    pl.ds(t * 8 + c4 * 2 + k2, n, stride=32), :
                ]


def assemble(received):
    out = pl.pallas_call(
        assemble_kernel,
        grid=(4,),
        out_shape=jax.ShapeDtypeStruct((2, 4, CHIPS, 512), jnp.float32),
        in_specs=[pl.BlockSpec((512, 128), lambda i: (i, 0))],
        out_specs=pl.BlockSpec((2, 4, 16, 512), lambda i: (0, 0, i, 0)),
        compiler_params=params(),
        name="assemble_sens",
    )(received)
    return out.reshape(2, 256, 512)

def exchange(parts):
    return lax.all_to_all(parts, "snode", 0, 0, tiled=True)


def local(leaf_rhs, top_rhs, leaf_inv, coupling, top_inv, cond, electrodes, blocks):
    me = lax.axis_index("snode").astype(jnp.int32).reshape(1)
    core = lax.axis_index("core").astype(jnp.int32).reshape(1)

    lists = [(electrodes.T * 2).reshape(16, 128), blocks.reshape(64, 128), jnp.zeros((48, 128), jnp.int32)]
    lists = jnp.concatenate(lists, axis=0).astype(jnp.float32)
    lists = lax.all_gather(lists, ("chip", "core"), axis=0, tiled=True)
    el = lists.reshape(8, 2, 128, 128)[:, :, :16]
    el = jnp.where(core[0] == 1, el[:, 1], el[:, 0]).astype(jnp.int32).reshape(8 * 2048)

    partial_value, forward = front(leaf_inv, leaf_rhs, coupling)
    coupled = exchange(partial_value.reshape(8, 256, 128))
    res = exchange(residual(me, coupled, top_rhs))
    separator = exchange(spread(exchange(top(top_inv, res))))

    send = back(separator, forward, coupling, leaf_inv, cond)
    own = lax.all_to_all(send.reshape(CHIPS, 32, 128), ("chip", "snode"), 0, 0, tiled=True)
    own = own.reshape(8, 256, 128)
    other = lax.ppermute(own, "core", [(0, 1), (1, 0)])
    picked = select(core, el, lists, own, other)
    received = lax.all_to_all(picked, ("chip", "snode"), 0, 0, tiled=True)
    return assemble(received.reshape(CHIPS * 32, 128))


def solution(mesh):
    devices = np.asarray(mesh.devices)
    fine = Mesh(devices.reshape(8, 2, 8), ("chip", "core", "snode"))
    src = ("chip", "core")
    return jax.shard_map(
        local,
        mesh=fine,
        in_specs=(
            P("snode", None, src),
            P(None, src),
            P("snode", None, None),
            P("snode", None, None),
            P("snode", None),
            P("snode", None),
            P(src, None),
            P(None, src),
        ),
        out_specs=P("snode", None, src),
        check_vma=False,
    )
```

time: 217 us -> 201 us (0.926)
  matrix products: 34 us -> 0 us
  Pallas kernels: 31.8 us -> 46.7 us
  waiting for transfers between devices: 26.2 us -> 36.7 us
  local copies, waits for them, and re-layouts: 11.7 us -> 7.33 us
  other arithmetic: 5.24 us -> 1.61 us
    dot_general x5 -> x0, matrix products: 34 us -> none  [the longest x1 17.1 us: local(): jnp.einsum('bti,ts->bis', coupling, separator_field, precision=HIGH)]
    pallas_call x3 -> x7, Pallas kernels: 31.8 us -> 46.7 us  [the longest x1 19.4 us: select(): pl.pallas_call(select_kernel, grid_spec=pltpu.PrefetchScalarGridSpec(num_...]
    all_gather x1, waiting for transfers between devices: 0.01 us -> 9.14 us  [local(): lists = lax.all_gather(lists, ('chip', 'core'), axis=0, tiled=True)]
    unnamed x13 -> x24, local copies, waits for them, and re-layouts: 0.14 us -> 7.24 us
    reshape x4 -> x2, local copies, waits for them, and re-layouts: 5.93 us -> 0.01 us  [the longest x1 0.01 us: local(): (electrodes.T * 2).reshape(16, 128)]
    all_to_all x1 -> x0, local copies, waits for them, and re-layouts: 2.8 us -> none  [all_gather(): lax.all_to_all(whole, 'snode', 0, 0, tiled=True)]
    reduce_sum x2 -> x0, other arithmetic: 2.62 us -> none  [reduce_scatter(): return jnp.sum(parts, axis=0)]
  transfers between devices with their start and end apart: 4 -> 4, of which waited for: 2 -> 3; matrix products, arithmetic and copies ran while one was open for 13% -> 1% of each run, Pallas kernels for 1% -> 6%
where the time goes in v2:
time: 201 us; the launch traced here: 200 us
  blocking collectives  84.4 us (42%)
  Pallas kernels  46.7 us (23%)
  waiting for transfers between devices  36.7 us (18%)
  between operations  13.5 us (7%)
  starting transfers between devices  9.64 us (5%)
  local copies, waits for them, and re-layouts  7.33 us (4%)
    all_to_all x2, blocking collectives, exchange(): return lax.all_to_all(parts, 'snode', 0, 0, tiled=True)  34 us
    all_to_all x2, waiting for transfers between devices, exchange(): return lax.all_to_all(parts, 'snode', 0, 0, tiled=True)  27.6 us
    all_to_all x1, blocking collectives, local(): lax.all_to_all(send.reshape(CHIPS, 32, 128), ('chip', 'snode'), 0, 0, til...  26.4 us
    all_to_all x1, blocking collectives, local(): received = lax.all_to_all(picked, ('chip', 'snode'), 0, 0, tiled=True)  23.9 us
    pallas_call x1, Pallas kernels, select(): pl.pallas_call(select_kernel, grid_spec=pltpu.PrefetchScalarGridSpec(num_...  19.4 us
    pallas_call x1, Pallas kernels, front(): pl.pallas_call(front_kernel, grid=(8,), out_shape=(jax.ShapeDtypeStruct((...  12.5 us
    pallas_call x1, Pallas kernels, back(): pl.pallas_call(back_kernel, grid=(8,), out_shape=jax.ShapeDtypeStruct((CH...  11.4 us
    all_to_all x2, starting transfers between devices, exchange(): return lax.all_to_all(parts, 'snode', 0, 0, tiled=True)  9.6 us
  transfers between devices with their start and end apart: 4, of which 3 were waited for; matrix products, arithmetic and copies ran while one was open for 1% of the time, Pallas kernels for 6%

profile of v2, /device:TPU:0, one launch (start us, length us, event | category | flops | bytes accessed | tf_op | source)
XLA Modules:
  0.0 199.9 jit_solution(8683336174394502360)
XLA Ops:
  6.5 1.6 copy-done
  8.1 1.2 copy-done.5
  9.4 12.5 %leaf_front.1 = (f32[2048,128]{1,0:T(8,128)}, f32[8,128,256]{2,1,0:T(8,128)S(1)}) custom-call(f32[8,256,256]{2,1,0:T(8,128)S(1)} %copy-done, f32[8,256,128]{2,1,0:T(8,128)S(1)} %copy-done.5, f32[8,2048,256]{2,1,0:T(8,128)} %coupling_ref.3), custom_call_target="tpu_custom_call" | custom-call | tf_op jit(solution)/shard_map/leaf_front/pallas_call | solution.py:49
  21.9 1.0 copy-done.6
  22.9 6.0 %all-to-all-start = ((f32[8,256,128]{2,1,0:T(8,128)}), f32[8,256,128]{2,1,0:T(8,128)S(1)}, u32[]{:S(2)}, u32[]{:S(2)}) async-start(f32[8,256,128]{2,1,0:T(8,128)} %bitcast.5), calls=%async_computation | async-start | bytes 2097152 | tf_op jit(solution)/shard_map/all_to_all | solution.py:290
  28.9 15.9 %all-to-all-done.parts_ref = f32[8,256,128]{2,1,0:T(8,128)S(1)} async-done(((f32[8,256,128]{2,1,0:T(8,128)}), f32[8,256,128]{2,1,0:T(8,128)S(1)}, u32[]{:S(2)}, u32[]{:S(2)}) %all-to-all-start) | async-done | bytes 1048608 | tf_op jit(solution)/shard_map/all_to_all | solution.py:290
  44.7 0.0 copy-done.8
  44.8 0.1 residual.1
  44.8 17.4 %all_to_all.30.res_ref = f32[8,256,128]{2,1,0:T(8,128)S(1)} all-to-all(f32[8,256,128]{2,1,0:T(8,128)S(1)} %residual.1), channel_id=1, replica_groups=mesh['chip'=8,'core'=2,'snode'=8] {'snode'}, dimensions={0} | all-to-all | bytes 2097152 | tf_op jit(solution)/shard_map/all_to_all | solution.py:290
  62.3 1.4 top_solve.1
  63.7 16.5 %all_to_all.31.parts_ref = f32[8,128,256]{2,1,0:T(8,128)S(1)} all-to-all(f32[8,128,256]{2,1,0:T(8,128)S(1)} %top_solve.1), channel_id=1, replica_groups=mesh['chip'=8,'core'=2,'snode'=8] {'snode'}, dimensions={0} | all-to-all | bytes 2097152 | tf_op jit(solution)/shard_map/all_to_all | solution.py:290
  80.2 0.1 spread.1
  80.3 0.0 copy-start.2
  80.3 1.0 copy-done.2
  81.3 3.6 %all-to-all-start.3 = ((f32[8,128,256]{2,1,0:T(8,128)}), f32[8,128,256]{2,1,0:T(8,128)S(1)}, u32[]{:S(2)}, u32[]{:S(2)}) async-start(f32[8,128,256]{2,1,0:T(8,128)} %copy-done.2), calls=%async_computation.3 | async-start | bytes 2097152 | tf_op jit(solution)/shard_map/all_to_all | solution.py:290
  84.8 0.0 all-gather.2.cloned.1.call-start
  85.0 0.1 pad.2.clone
  85.0 0.7 add_convert_fusion
  85.8 0.0 all-gather.2.cloned.1.call-update
  85.8 11.7 %all-to-all-done.3.sep_ref = f32[8,128,256]{2,1,0:T(8,128)S(1)} async-done(((f32[8,128,256]{2,1,0:T(8,128)}), f32[8,128,256]{2,1,0:T(8,128)S(1)}, u32[]{:S(2)}, u32[]{:S(2)}) %all-to-all-start.3) | async-done | bytes 1048608 | tf_op jit(solution)/shard_map/all_to_all | solution.py:290
  97.5 0.0 copy-done.9
  97.5 1.2 copy-done.7
  98.7 11.4 %leaf_back.1 = f32[2048,128]{1,0:T(8,128)S(1)} custom-call(f32[8,128,256]{2,1,0:T(8,128)S(1)} %all-to-all-done.3.sep_ref, f32[8,128,256]{2,1,0:T(8,128)S(1)} %copy-done.7, f32[8,2048,256]{2,1,0:T(8,128)} %coupling_ref.3, f32[8,256,256]{2,1,0:T(8,128)S(1)} %copy-done.1, f32[8,256]{1,0:T(8,128)S(1)} %copy-done.9), custom_call_target="tpu_custom_call" | custom-call | tf_op jit(solution)/shard_map/leaf_back/pallas_call | solution.py:169
  110.1 26.4 %all_to_all.32 = f32[64,32,128]{2,1,0:T(8,128)S(1)} all-to-all(f32[64,32,128]{2,1,0:T(8,128)S(1)} %bitcast.13), channel_id=1, replica_groups=mesh['chip'=8,'core'=2,'snode'=8] {'chip','snode'}, dimensions={0} | all-to-all | bytes 2097152 | tf_op jit(solution)/shard_map/all_to_all | solution.py:309
  136.6 0.0 collective-permute-start
  136.6 9.1 %all-gather.2.cloned.1.call-done.lists_ref = f32[2048,128]{1,0:T(8,128)} async-done(((f32[128,128]{1,0:T(8,128)}), f32[2048,128]{1,0:T(8,128)}) %all-gather.2.cloned.1.call-update) | async-done | bytes 1048592 | tf_op jit(solution)/shard_map/all_gather | solution.py:299
  145.7 0.9 fusion
  146.6 0.0 collective-permute-done.other_ref
  146.6 1.2 copy-done.4
  147.8 19.4 %select_quads.1 = f32[64,32,128]{2,1,0:T(8,128)S(1)} custom-call(s32[1]{0:T(128)} %bitcast.core_ref, s32[16384]{0:T(1024)S(1)} %bitcast.16, f32[2048,128]{1,0:T(8,128)S(1)} %copy-done.4, f32[8,256,128]{2,1,0:T(8,128)S(1)} %bitcast.12, f32[8,256,128]{2,1,0:T(8,128)S(1)} %collective-permute-done.other_ref), custom_call_target="tpu_custom_call" | custom-call | tf_op jit(solution)/shard_map/select_quads/pallas_call | solution.py:243
  167.2 23.9 %all_to_all.33 = f32[64,32,128]{2,1,0:T(8,128)S(1)} all-to-all(f32[64,32,128]{2,1,0:T(8,128)S(1)} %select_quads.1), channel_id=1, replica_groups=mesh['chip'=8,'core'=2,'snode'=8] {'chip','snode'}, dimensions={0} | all-to-all | bytes 2097152 | tf_op jit(solution)/shard_map/all_to_all | solution.py:313
  191.1 1.9 assemble_sens.1
  (19 shorter events, 0.0 us)
Async XLA Ops:
  6.5 1.6 copy-start
  8.1 1.2 copy-start.5
  21.9 1.0 copy-start.6
  22.9 21.9 %copy-start.8 = (f32[2048,128]{1,0:T(8,128)S(1)}, f32[2048,128]{1,0:T(8,128)}, u32[]{:S(2)}) copy-start(f32[2048,128]{1,0:T(8,128)} %top_ref.1) | copy-start | bytes 3145732
  22.9 21.9 %all-to-all-start = ((f32[8,256,128]{2,1,0:T(8,128)}), f32[8,256,128]{2,1,0:T(8,128)S(1)}, u32[]{:S(2)}, u32[]{:S(2)}) async-start(f32[8,256,128]{2,1,0:T(8,128)} %bitcast.5), calls=%async_computation | async-start | bytes 2097152 | tf_op jit(solution)/shard_map/all_to_all | solution.py:290
  44.8 17.5 %copy-start.3 = (f32[256,2048]{1,0:T(8,128)S(1)}, f32[256,2048]{1,0:T(8,128)}, u32[]{:S(2)}) copy-start(f32[256,2048]{1,0:T(8,128)} %inv_ref.4) | copy-start | bytes 6291460
  80.2 4.7 %copy-start.10 = (s32[16,512]{1,0:T(8,128)S(1)}, s32[16,512]{1,0:T(8,128)}, u32[]{:S(2)}) copy-start(s32[16,512]{1,0:T(8,128)} %param.15) | copy-start | bytes 98308
  80.2 4.7 %copy-start.11 = (s32[512,4]{0,1:T(4,128)S(1)}, s32[512,4]{0,1:T(4,128)}, u32[]{:S(2)}) copy-start(s32[512,4]{0,1:T(4,128)} %param.14) | copy-start | bytes 24580
  80.2 17.3 %copy-start.1 = (f32[8,256,256]{2,1,0:T(8,128)S(1)}, f32[8,256,256]{2,1,0:T(8,128)}, u32[]{:S(2)}) copy-start(f32[8,256,256]{2,1,0:T(8,128)} %inv_ref.5) | copy-start | bytes 6291460
  80.2 17.3 %copy-start.9 = (f32[8,256]{1,0:T(8,128)S(1)}, f32[8,256]{1,0:T(8,128)}, u32[]{:S(2)}) copy-start(f32[8,256]{1,0:T(8,128)} %cond_ref.1) | copy-start | bytes 24580
  80.3 1.0 copy-start.2
  81.3 16.2 %all-to-all-start.3 = ((f32[8,128,256]{2,1,0:T(8,128)}), f32[8,128,256]{2,1,0:T(8,128)S(1)}, u32[]{:S(2)}, u32[]{:S(2)}) async-start(f32[8,128,256]{2,1,0:T(8,128)} %copy-done.2), calls=%async_computation.3 | async-start | bytes 2097152 | tf_op jit(solution)/shard_map/all_to_all | solution.py:290
  84.8 60.9 %all-gather.2.cloned.1.call-start = ((), (), s32[]{:S(2)}) async-start(), calls=%async_computation.6 | async-start | bytes 1114112 | tf_op jit(solution)/shard_map/all_gather | solution.py:299
  97.5 1.2 copy-start.7
  136.6 10.0 %collective-permute-start = (f32[8,256,128]{2,1,0:T(8,128)S(1)}, f32[8,256,128]{2,1,0:T(8,128)S(1)}, u32[]{:S(2)}, u32[]{:S(2)}) collective-permute-start(f32[8,256,128]{2,1,0:T(8,128)S(1)} %bitcast.11), channel_id=1, source_target_pairs={{0,8},{8,0},{1,9},{9,1},{2,10},{10,2},{3,11},{11,3},{4,12},{12,4},... | collective-permute-start | bytes 3145736 | tf_op jit(solution)/shard_map/ppermute | solution.py:311
  146.6 1.2 copy-start.4
Sparse Core Ops, SparseCore 0:
  88.1 57.5 all-gather.1

commit v3 on v2

--- a/solution.py
+++ b/solution.py
@@ -19,8 +19,11 @@
     return jnp.dot(a, b, preferred_element_type=jnp.float32)
 
 
-def params():
-    return pltpu.CompilerParams(vmem_limit_bytes=40 << 20)
+def params(mib):
+    return pltpu.CompilerParams(vmem_limit_bytes=mib << 20)
+
+
+PANEL = jax.ShapeDtypeStruct((256, 128), jnp.float32)
 
 
 def front_kernel(inv_ref, rhs_ref, coupling_ref, sum_ref, forward_ref):
@@ -62,59 +65,50 @@
             pl.BlockSpec((2048, 128), lambda j: (0, 0)),
             pl.BlockSpec((1, 128, 256), lambda j: (j, 0, 0)),
         ),
-        compiler_params=params(),
+        compiler_params=params(60),
         name="leaf_front",
     )(inv, rhs, coupling)
 
 
-def residual_kernel(me_ref, parts_ref, top_ref, out_ref):
+def residual_kernel(top_ref, parts_ref, out_ref):
     value = top_ref[...]
     for p in range(8):
         value = value - parts_ref[p]
-    for p in range(8):
-        out_ref[p] = value
-
-
-def residual(me, parts, top):
+    out_ref[...] = value
+
+
+def residual(top, parts):
     return pl.pallas_call(
         residual_kernel,
-        grid_spec=pltpu.PrefetchScalarGridSpec(
-            num_scalar_prefetch=1,
-            grid=(1,),
-            in_specs=[
-                pl.BlockSpec((8, 256, 128), lambda i, me: (0, 0, 0)),
-                pl.BlockSpec((256, 128), lambda i, me: (me[0], 0)),
-            ],
-            out_specs=pl.BlockSpec((8, 256, 128), lambda i, me: (0, 0, 0)),
-        ),
-        out_shape=jax.ShapeDtypeStruct((8, 256, 128), jnp.float32),
-        compiler_params=params(),
+        out_shape=PANEL,
+        compiler_params=params(16),
         name="residual",
-    )(me, parts, top)
-
-
-def spread_kernel(parts_ref, out_ref):
+    )(top, parts)
+
+
+def total_kernel(parts_ref, out_ref):
     value = parts_ref[0]
     for p in range(1, 8):
         value = value + parts_ref[p]
-    for p in range(8):
-        out_ref[p] = value
-
-
-def spread(parts):
-    return pl.pallas_call(
-        spread_kernel,
-        out_shape=jax.ShapeDtypeStruct(parts.shape, jnp.float32),
-        compiler_params=params(),
-        name="spread",
+    out_ref[...] = value
+
+
+def total(parts):
+    return pl.pallas_call(
+        total_kernel,
+        out_shape=jax.ShapeDtypeStruct((128, 256), jnp.float32),
+        compiler_params=params(16),
+        name="separator",
     )(parts)
 
 
-def top_kernel(inv_ref, res_ref, out_ref):
+def top_kernel(me_ref, inv_ref, *refs):
+    res, out_ref = refs[:8], refs[8]
     total = None
-    for p in range(8):
-        th, tl = two(inv_ref[:, p * 256 : (p + 1) * 256])
-        rh, rl = two(res_ref[p])
+    for d in range(8):
+        p = (me_ref[0] ^ (d // 2)) * 2 + (me_ref[1] ^ (d % 2))
+        th, tl = two(inv_ref[:, pl.ds(pl.multiple_of(p * 256, 256), 256)])
+        rh, rl = two(res[d][...])
         wide = mm(th, jnp.concatenate([rh, rl], axis=1))
         term = wide[:, :128] + wide[:, 128:] + mm(tl, rh)
         total = term if total is None else total + term
@@ -126,22 +120,31 @@
         out_ref[p] = wide[:128] + wide[128:] + mm(fh, tl)
 
 
-def top(inv, res):
+def top(me, inv, res):
     return pl.pallas_call(
         top_kernel,
+        grid_spec=pltpu.PrefetchScalarGridSpec(
+            num_scalar_prefetch=1,
+            grid=(1,),
+            in_specs=[pl.BlockSpec((256, 2048), lambda i, me: (0, 0))]
+            + [pl.BlockSpec((256, 128), lambda i, me: (0, 0))] * 8,
+            out_specs=pl.BlockSpec((8, 128, 256), lambda i, me: (0, 0, 0)),
+        ),
         out_shape=jax.ShapeDtypeStruct((8, 128, 256), jnp.float32),
-        compiler_params=params(),
+        compiler_params=params(24),
         name="top_solve",
-    )(inv, res)
-
-
-def back_kernel(sep_ref, forward_ref, coupling_ref, inv_ref, cond_ref, out_ref, split_ref, total_ref):
+    )(me, inv, *res)
+
+
+def back_kernel(me_ref, *refs):
+    sep, (forward_ref, coupling_ref, inv_ref, cond_ref, out_ref, split_ref, total_ref) = refs[:8], refs[8:]
     j = pl.program_id(0)
 
     @pl.when(j == 0)
     def _():
-        for p in range(8):
-            split_ref[p, :128], split_ref[p, 128:] = two(sep_ref[p])
+        for d in range(8):
+            p = (me_ref[0] ^ (d // 2)) * 2 + (me_ref[1] ^ (d % 2))
+            split_ref[p, :128], split_ref[p, 128:] = two(sep[d][...])
 
     total = forward_ref[0]
     for p in range(8):
@@ -165,29 +168,32 @@
                 out_ref[pl.ds(row, CHIPS, stride=32), :] = field[c4 * CHIPS : (c4 + 1) * CHIPS, :]
 
 
-def back(sep, forward, coupling, inv, cond):
+def back(me, sep, forward, coupling, inv, cond):
     return pl.pallas_call(
         back_kernel,
-        grid=(8,),
+        grid_spec=pltpu.PrefetchScalarGridSpec(
+            num_scalar_prefetch=1,
+            grid=(8,),
+            in_specs=[pl.BlockSpec((128, 256), lambda j, me: (0, 0))] * 8
+            + [
+                pl.BlockSpec((1, 128, 256), lambda j, me: (j, 0, 0)),
+                pl.BlockSpec((1, 2048, 256), lambda j, me: (j, 0, 0)),
+                pl.BlockSpec((8, 256, 256), lambda j, me: (0, 0, 0)),
+                pl.BlockSpec((8, 256), lambda j, me: (0, 0)),
+            ],
+            out_specs=pl.BlockSpec((CHIPS * 32, 128), lambda j, me: (0, 0)),
+            scratch_shapes=[
+                pltpu.VMEM((8, 256, 256), jnp.bfloat16),
+                pltpu.VMEM((8, 128, 256), jnp.float32),
+            ],
+        ),
         out_shape=jax.ShapeDtypeStruct((CHIPS * 32, 128), jnp.float32),
-        in_specs=[
-            pl.BlockSpec((8, 128, 256), lambda j: (0, 0, 0)),
-            pl.BlockSpec((1, 128, 256), lambda j: (j, 0, 0)),
-            pl.BlockSpec((1, 2048, 256), lambda j: (j, 0, 0)),
-            pl.BlockSpec((8, 256, 256), lambda j: (0, 0, 0)),
-            pl.BlockSpec((8, 256), lambda j: (0, 0)),
-        ],
-        out_specs=pl.BlockSpec((CHIPS * 32, 128), lambda j: (0, 0)),
-        scratch_shapes=[
-            pltpu.VMEM((8, 256, 256), jnp.bfloat16),
-            pltpu.VMEM((8, 128, 256), jnp.float32),
-        ],
-        compiler_params=params(),
+        compiler_params=params(48),
         name="leaf_back",
-    )(sep, forward, coupling, inv, cond)
-
-
-def select_kernel(core_ref, el_ref, lists_ref, own_ref, other_ref, out_ref, rows_ref, prod_ref, ids_ref):
+    )(me, *sep, forward, coupling, inv, cond)
+
+
+def select_kernel(core_ref, el_ref, lists_ref, own_ref, other_ref, out_ref, rows_ref, prod_ref, ids_ref, lanes_ref):
     @pl.when(pl.program_id(0) == 0)
     def _():
         for chip in range(8):
@@ -220,9 +226,10 @@
     upper = lane & 4 != 0
     for pair in range(2):
         for t2 in range(2):
+            at = (pair * 2 + t2) * 128
+            lanes_ref[...] = lists_ref[:16, at : at + 128].astype(jnp.int32) * 2
             for k2 in range(2):
-                at = 16 + k2 * 4 + pair * 2 + t2
-                lanes = lists_ref[pl.ds(at, 8, stride=8), :].astype(jnp.int32) * 2
+                lanes = lanes_ref[pl.ds(k2, 8, stride=2), :]
                 for c2 in range(2):
                     for half in range(2):
                         ids_ref[pl.ds(t2 * 8 + half * 4 + c2 * 2 + k2, 8, stride=16), :] = lanes + c2
@@ -247,7 +254,7 @@
             grid=(8,),
             in_specs=[
                 pl.BlockSpec((2048,), lambda i, core: (i,), memory_space=pltpu.SMEM),
-                pl.BlockSpec((128, 128), lambda i, core: (2 * i + core[0], 0)),
+                pl.BlockSpec((32, 512), lambda i, core: (2 * i + core[0], 0)),
                 pl.BlockSpec((8, 256, 128), lambda i, core: (0, 0, 0)),
                 pl.BlockSpec((8, 256, 128), lambda i, core: (0, 0, 0)),
             ],
@@ -256,10 +263,11 @@
                 pltpu.VMEM((4096, 128), jnp.float32),
                 pltpu.VMEM((1024, 128), jnp.float32),
                 pltpu.VMEM((128, 128), jnp.int32),
+                pltpu.VMEM((16, 128), jnp.int32),
             ],
         ),
         out_shape=jax.ShapeDtypeStruct((CHIPS, 32, 128), jnp.float32),
-        compiler_params=params(),
+        compiler_params=params(24),
         name="select_quads",
     )(core, el, lists, own, other)
 
@@ -281,56 +289,73 @@
         out_shape=jax.ShapeDtypeStruct((2, 4, CHIPS, 512), jnp.float32),
         in_specs=[pl.BlockSpec((512, 128), lambda i: (i, 0))],
         out_specs=pl.BlockSpec((2, 4, 16, 512), lambda i: (0, 0, i, 0)),
-        compiler_params=params(),
+        compiler_params=params(16),
         name="assemble_sens",
     )(received)
     return out.reshape(2, 256, 512)
 
 def exchange(parts):
-    return lax.all_to_all(parts, "snode", 0, 0, tiled=True)
+    return lax.all_to_all(parts, ("y", "z"), 0, 0, tiled=True)
+
+
+def send(value, d):
+    return lax.ppermute(value, ("y", "z"), [(i, i ^ d) for i in range(8)])
+
+
+def swap(value, axis):
+    return lax.ppermute(value, axis, [(0, 1), (1, 0)])
+
+
+def all_panels(own):
+    far = swap(own, "z")
+    return [send(value, 2 * dy) if dy else value for dy in range(4) for value in (own, far)]
 
 
 def local(leaf_rhs, top_rhs, leaf_inv, coupling, top_inv, cond, electrodes, blocks):
-    me = lax.axis_index("snode").astype(jnp.int32).reshape(1)
+    me = jnp.stack([lax.axis_index("y"), lax.axis_index("z")]).astype(jnp.int32)
     core = lax.axis_index("core").astype(jnp.int32).reshape(1)
 
-    lists = [(electrodes.T * 2).reshape(16, 128), blocks.reshape(64, 128), jnp.zeros((48, 128), jnp.int32)]
+    partial_value, forward = front(leaf_inv, leaf_rhs, coupling)
+    electrodes, blocks, partial_value = lax.optimization_barrier((electrodes, blocks, partial_value))
+    lists = [blocks, electrodes.T * 2, jnp.zeros((12, 512), jnp.int32)]
     lists = jnp.concatenate(lists, axis=0).astype(jnp.float32)
     lists = lax.all_gather(lists, ("chip", "core"), axis=0, tiled=True)
-    el = lists.reshape(8, 2, 128, 128)[:, :, :16]
+    el = lists.reshape(8, 2, 32, 512)[:, :, 16:20]
     el = jnp.where(core[0] == 1, el[:, 1], el[:, 0]).astype(jnp.int32).reshape(8 * 2048)
 
-    partial_value, forward = front(leaf_inv, leaf_rhs, coupling)
-    coupled = exchange(partial_value.reshape(8, 256, 128))
-    res = exchange(residual(me, coupled, top_rhs))
-    separator = exchange(spread(exchange(top(top_inv, res))))
-
-    send = back(separator, forward, coupling, leaf_inv, cond)
-    own = lax.all_to_all(send.reshape(CHIPS, 32, 128), ("chip", "snode"), 0, 0, tiled=True)
+    at = (me[0] * 2 + me[1]) * 256
+    top_own = lax.dynamic_slice_in_dim(top_rhs, at, 256, 0)
+    res = residual(top_own, exchange(partial_value.reshape(8, 256, 128)))
+    separator = all_panels(total(exchange(top(me, top_inv, all_panels(res)))))
+    separator, el, lists = lax.optimization_barrier((separator, el, lists))
+
+    fields = back(me, separator, forward, coupling, leaf_inv, cond)
+    own = lax.all_to_all(fields.reshape(CHIPS, 32, 128), ("chip", "y", "z"), 0, 0, tiled=True)
     own = own.reshape(8, 256, 128)
     other = lax.ppermute(own, "core", [(0, 1), (1, 0)])
     picked = select(core, el, lists, own, other)
-    received = lax.all_to_all(picked, ("chip", "snode"), 0, 0, tiled=True)
+    received = lax.all_to_all(picked, ("chip", "y", "z"), 0, 0, tiled=True)
     return assemble(received.reshape(CHIPS * 32, 128))
 
 
 def solution(mesh):
     devices = np.asarray(mesh.devices)
-    fine = Mesh(devices.reshape(8, 2, 8), ("chip", "core", "snode"))
+    fine = Mesh(devices.reshape(8, 2, 4, 2), ("chip", "core", "y", "z"))
     src = ("chip", "core")
+    snode = ("y", "z")
     return jax.shard_map(
         local,
         mesh=fine,
         in_specs=(
-            P("snode", None, src),
+            P(snode, None, src),
             P(None, src),
-            P("snode", None, None),
-            P("snode", None, None),
-            P("snode", None),
-            P("snode", None),
+            P(snode, None, None),
+            P(snode, None, None),
+            P(snode, None),
+            P(snode, None),
             P(src, None),
             P(None, src),
         ),
-        out_specs=P("snode", None, src),
+        out_specs=P(snode, None, src),
         check_vma=False,
     )

time: 201 us -> 192 us (0.955)
  starting transfers between devices: 9.64 us -> 27 us
  blocking collectives: 84.4 us -> 68.7 us
  waiting for transfers between devices: 36.7 us -> 28.4 us
  local copies, waits for them, and re-layouts: 7.33 us -> 2.96 us
    ppermute x0 -> x14, starting transfers between devices: none -> 20.9 us  [the longest x12 18.8 us: send(): return lax.ppermute(value, ('y', 'z'), [(i, i ^ d) for i in range(8)])]
    all_to_all x4 -> x3, blocking collectives: 84.4 us -> 68.7 us  [the longest x1 26.3 us: local(): lax.all_to_all(fields.reshape(CHIPS, 32, 128), ('chip', 'y', 'z'), 0, 0,...]
    all_to_all x2 -> x1, waiting for transfers between devices: 27.6 us -> 14.9 us  [exchange(): return lax.all_to_all(parts, ('y', 'z'), 0, 0, tiled=True)]
    ppermute x0 -> x14, waiting for transfers between devices: none -> 10.8 us  [the longest x12 10.8 us: send(): return lax.ppermute(value, ('y', 'z'), [(i, i ^ d) for i in range(8)])]
    all_gather x1, waiting for transfers between devices: 9.14 us -> 0.01 us  [local(): lists = lax.all_gather(lists, ('chip', 'core'), axis=0, tiled=True)]
    unnamed x24 -> x17, local copies, waits for them, and re-layouts: 7.24 us -> 2.86 us
    all_to_all x2 -> x1, starting transfers between devices: 9.6 us -> 6.05 us  [exchange(): return lax.all_to_all(parts, ('y', 'z'), 0, 0, tiled=True)]
    ppermute x1, waiting for transfers between devices: 0.01 us -> 2.66 us  [local(): other = lax.ppermute(own, 'core', [(0, 1), (1, 0)])]
  transfers between devices with their start and end apart: 4 -> 17, of which waited for: 3 -> 6; matrix products, arithmetic and copies ran while one was open for 1% -> 1% of each run, Pallas kernels for 6% -> 1%
where the time goes in v3:
time: 192 us; the launch traced here: 191 us
  blocking collectives  68.7 us (36%)
  Pallas kernels  48.6 us (25%)
  waiting for transfers between devices  28.4 us (15%)
  starting transfers between devices  27 us (14%)
  between operations  13.5 us (7%)
  local copies, waits for them, and re-layouts  2.96 us (2%)
    all_to_all x1, blocking collectives, local(): lax.all_to_all(fields.reshape(CHIPS, 32, 128), ('chip', 'y', 'z'), 0, 0,...  26.3 us
    all_to_all x1, blocking collectives, local(): received = lax.all_to_all(picked, ('chip', 'y', 'z'), 0, 0, tiled=True)  23.7 us
    pallas_call x1, Pallas kernels, select(): pl.pallas_call(select_kernel, grid_spec=pltpu.PrefetchScalarGridSpec(num_...  19.4 us
    ppermute x12, starting transfers between devices, send(): return lax.ppermute(value, ('y', 'z'), [(i, i ^ d) for i in range(8)])  18.8 us
    all_to_all x1, blocking collectives, exchange(): return lax.all_to_all(parts, ('y', 'z'), 0, 0, tiled=True)  18.7 us
    all_to_all x1, waiting for transfers between devices, exchange(): return lax.all_to_all(parts, ('y', 'z'), 0, 0, tiled=True)  14.9 us
    pallas_call x1, Pallas kernels, front(): pl.pallas_call(front_kernel, grid=(8,), out_shape=(jax.ShapeDtypeStruct((...  13.2 us
    pallas_call x1, Pallas kernels, back(): pl.pallas_call(back_kernel, grid_spec=pltpu.PrefetchScalarGridSpec(num_sc...  12.1 us
  transfers between devices with their start and end apart: 17, of which 6 were waited for; matrix products, arithmetic and copies ran while one was open for 1% of the time, Pallas kernels for 1%

profile of v3, /device:TPU:0, one launch (start us, length us, event | category | flops | bytes accessed | tf_op | source)
XLA Modules:
  0.0 190.9 jit_solution(13659858675531700180)
XLA Ops:
  6.5 13.2 %leaf_front.1 = (f32[2048,128]{1,0:T(8,128)}, f32[8,128,256]{2,1,0:T(8,128)}) custom-call(f32[8,256,256]{2,1,0:T(8,128)} %refs_10_.1, f32[8,256,128]{2,1,0:T(8,128)} %rhs_ref.1, f32[8,2048,256]{2,1,0:T(8,128)} %refs_9_.1), custom_call_target="tpu_custom_call" | custom-call | tf_op jit(solution)/shard_map/leaf_front/pallas_call | solution.py:52
  19.8 6.1 %all-to-all-start = ((f32[8,256,128]{2,1,0:T(8,128)}), f32[8,256,128]{2,1,0:T(8,128)S(1)}, u32[]{:S(2)}, u32[]{:S(2)}) async-start(f32[8,256,128]{2,1,0:T(8,128)} %bitcast.20), calls=%async_computation | async-start | bytes 2097152 | tf_op jit(solution)/shard_map/all_to_all | solution.py:298
  26.0 0.7 add_convert_fusion
  26.7 14.9 %all-to-all-done.parts_ref = f32[8,256,128]{2,1,0:T(8,128)S(1)} async-done(((f32[8,256,128]{2,1,0:T(8,128)}), f32[8,256,128]{2,1,0:T(8,128)S(1)}, u32[]{:S(2)}, u32[]{:S(2)}) %all-to-all-start) | async-done | bytes 1048608 | tf_op jit(solution)/shard_map/all_to_all | solution.py:298
  41.7 0.8 collective-permute-start
  42.6 0.6 collective-permute-start.1
  43.1 2.1 %collective-permute-start.3 = (f32[256,128]{1,0:T(8,128)S(1)}, f32[256,128]{1,0:T(8,128)S(1)}, u32[]{:S(2)}, u32[]{:S(2)}) collective-permute-start(f32[256,128]{1,0:T(8,128)S(1)} %residual.1.refs_0_), channel_id=1, source_target_pairs={{0,4},{1,5},{2,6},{3,7},{4,0},{5,1},{6,2},{7,3},{8,12},{9,13},{10,... | collective-permute-start | bytes 393224 | tf_op jit(solution)/shard_map/ppermute | solution.py:302
  45.2 2.1 %collective-permute-start.5 = (f32[256,128]{1,0:T(8,128)S(1)}, f32[256,128]{1,0:T(8,128)S(1)}, u32[]{:S(2)}, u32[]{:S(2)}) collective-permute-start(f32[256,128]{1,0:T(8,128)S(1)} %residual.1.refs_0_), channel_id=1, source_target_pairs={{0,6},{1,7},{2,4},{3,5},{4,2},{5,3},{6,0},{7,1},{8,14},{9,15},{10,... | collective-permute-start | bytes 393224 | tf_op jit(solution)/shard_map/ppermute | solution.py:302
  47.3 0.4 collective-permute-start.2
  47.6 2.3 %collective-permute-start.4 = (f32[256,128]{1,0:T(8,128)S(1)}, f32[256,128]{1,0:T(8,128)S(1)}, u32[]{:S(2)}, u32[]{:S(2)}) collective-permute-start(f32[256,128]{1,0:T(8,128)S(1)} %collective-permute-done.refs_1_), channel_id=1, source_target_pairs={{0,4},{1,5},{2,6},{3,7},{4,0},{5,1},{6,2},{7,3},{8,12},{9,13},{10,... | collective-permute-start | bytes 393224 | tf_op jit(solution)/shard_map/ppermute | solution.py:302
  49.9 2.1 %collective-permute-start.6 = (f32[256,128]{1,0:T(8,128)S(1)}, f32[256,128]{1,0:T(8,128)S(1)}, u32[]{:S(2)}, u32[]{:S(2)}) collective-permute-start(f32[256,128]{1,0:T(8,128)S(1)} %collective-permute-done.refs_1_), channel_id=1, source_target_pairs={{0,6},{1,7},{2,4},{3,5},{4,2},{5,3},{6,0},{7,1},{8,14},{9,15},{10,... | collective-permute-start | bytes 393224 | tf_op jit(solution)/shard_map/ppermute | solution.py:302
  52.0 3.9 %collective-permute-done.5.refs_6_ = f32[256,128]{1,0:T(8,128)S(1)} collective-permute-done((f32[256,128]{1,0:T(8,128)S(1)}, f32[256,128]{1,0:T(8,128)S(1)}, u32[]{:S(2)}, u32[]{:S(2)}) %collective-permute-start.5) | collective-permute-done | bytes 131104 | tf_op jit(solution)/shard_map/ppermute | solution.py:302
  56.0 1.8 collective-permute-done.6.refs_7_
  57.8 1.6 copy-done.2
  59.4 1.9 top_solve.1
  61.3 18.7 %all_to_all.20.parts_ref = f32[8,128,256]{2,1,0:T(8,128)S(1)} all-to-all(f32[8,128,256]{2,1,0:T(8,128)S(1)} %top_solve.1), channel_id=1, replica_groups=mesh['chip'=8,'core'=2,'y'=4,'z'=2] {'y','z'}, dimensions={0} | all-to-all | bytes 2097152 | tf_op jit(solution)/shard_map/all_to_all | solution.py:298
  80.0 1.3 collective-permute-start.7
  81.3 0.6 collective-permute-start.8
  81.9 2.1 %collective-permute-start.10 = (f32[128,256]{1,0:T(8,128)S(1)}, f32[128,256]{1,0:T(8,128)}, u32[]{:S(2)}, u32[]{:S(2)}) collective-permute-start(f32[128,256]{1,0:T(8,128)S(1)} %separator.1.refs_0_), channel_id=1, source_target_pairs={{0,4},{1,5},{2,6},{3,7},{4,0},{5,1},{6,2},{7,3},{8,12},{9,13},{10,... | collective-permute-start | bytes 393224 | tf_op jit(solution)/shard_map/ppermute | solution.py:302
  84.0 2.1 %collective-permute-start.12 = (f32[128,256]{1,0:T(8,128)S(1)}, f32[128,256]{1,0:T(8,128)}, u32[]{:S(2)}, u32[]{:S(2)}) collective-permute-start(f32[128,256]{1,0:T(8,128)S(1)} %separator.1.refs_0_), channel_id=1, source_target_pairs={{0,6},{1,7},{2,4},{3,5},{4,2},{5,3},{6,0},{7,1},{8,14},{9,15},{10,... | collective-permute-start | bytes 393224 | tf_op jit(solution)/shard_map/ppermute | solution.py:302
  86.0 2.6 %collective-permute-start.11 = (f32[128,256]{1,0:T(8,128)S(1)}, f32[128,256]{1,0:T(8,128)}, u32[]{:S(2)}, u32[]{:S(2)}) collective-permute-start(f32[128,256]{1,0:T(8,128)S(1)} %collective-permute-done.7.refs_1_), channel_id=1, source_target_pairs={{0,4},{1,5},{2,6},{3,7},{4,0},{5,1},{6,2},{7,3},{8,12},{9,13},{10,... | collective-permute-start | bytes 393224 | tf_op jit(solution)/shard_map/ppermute | solution.py:302
  88.7 2.1 %collective-permute-start.13 = (f32[128,256]{1,0:T(8,128)S(1)}, f32[128,256]{1,0:T(8,128)}, u32[]{:S(2)}, u32[]{:S(2)}) collective-permute-start(f32[128,256]{1,0:T(8,128)S(1)} %collective-permute-done.7.refs_1_), channel_id=1, source_target_pairs={{0,6},{1,7},{2,4},{3,5},{4,2},{5,3},{6,0},{7,1},{8,14},{9,15},{10,... | collective-permute-start | bytes 393224 | tf_op jit(solution)/shard_map/ppermute | solution.py:302
  90.7 1.0 fusion.1
  91.8 3.6 %collective-permute-done.12.refs_6_ = f32[128,256]{1,0:T(8,128)} collective-permute-done((f32[128,256]{1,0:T(8,128)S(1)}, f32[128,256]{1,0:T(8,128)}, u32[]{:S(2)}, u32[]{:S(2)}) %collective-permute-start.12) | collective-permute-done | bytes 131104 | tf_op jit(solution)/shard_map/ppermute | solution.py:302
  95.4 1.4 collective-permute-done.13.refs_7_
  96.8 1.2 copy-done.4
  98.0 12.1 %leaf_back.1 = f32[2048,128]{1,0:T(8,128)S(1)} custom-call(s32[2]{0:T(128)S(1)} %pad_add_fusion.me_ref, f32[128,256]{1,0:T(8,128)S(1)} %separator.1.refs_0_, f32[128,256]{1,0:T(8,128)S(1)} %collective-permute-done.7.refs_1_, f32[128,256]{1,0:T(8,128)S(1)} %collective-permute-done.8.refs_2_, f32[128,256]{1,0:T(8,128)} %collective-permute-done.9.refs_3_, ...), custom_call_target="tpu_custom_call" | custom-call | tf_op jit(solution)/shard_map/leaf_back/pallas_call | solution.py:172
  110.1 26.3 %all_to_all.21 = f32[64,32,128]{2,1,0:T(8,128)S(1)} all-to-all(f32[64,32,128]{2,1,0:T(8,128)S(1)} %bitcast.16), channel_id=1, replica_groups=mesh['chip'=8,'core'=2,'y'=4,'z'=2] {'chip','y','z'}, dimensions={0} | all-to-all | bytes 2097152 | tf_op jit(solution)/shard_map/all_to_all | solution.py:333
  136.4 2.7 %collective-permute-done.14.other_ref = f32[8,256,128]{2,1,0:T(8,128)S(1)} collective-permute-done((f32[8,256,128]{2,1,0:T(8,128)S(1)}, f32[8,256,128]{2,1,0:T(8,128)S(1)}, u32[]{:S(2)}, u32[]{:S(2)}) %collective-permute-start.14) | collective-permute-done | bytes 1048608 | tf_op jit(solution)/shard_map/ppermute | solution.py:335
  139.1 19.4 %select_quads.1 = f32[64,32,128]{2,1,0:T(8,128)S(1)} custom-call(s32[1]{0:T(128)} %bitcast.core_ref, s32[16384]{0:T(1024)S(1)} %bitcast.19, f32[512,512]{1,0:T(8,128)S(1)} %copy-done.3, f32[8,256,128]{2,1,0:T(8,128)S(1)} %bitcast.15, f32[8,256,128]{2,1,0:T(8,128)S(1)} %collective-permute-done.14.other_ref), custom_call_target="tpu_custom_call" | custom-call | tf_op jit(solution)/shard_map/select_quads/pallas_call | solution.py:250
  158.5 23.7 %all_to_all.22 = f32[64,32,128]{2,1,0:T(8,128)S(1)} all-to-all(f32[64,32,128]{2,1,0:T(8,128)S(1)} %select_quads.1), channel_id=1, replica_groups=mesh['chip'=8,'core'=2,'y'=4,'z'=2] {'chip','y','z'}, dimensions={0} | all-to-all | bytes 2097152 | tf_op jit(solution)/shard_map/all_to_all | solution.py:337
  182.2 1.9 assemble_sens.1
  (37 shorter events, 0.4 us)
Async XLA Ops:
  6.5 20.2 %copy-start = (f32[2048,128]{1,0:T(8,128)S(1)}, f32[2048,128]{1,0:T(8,128)}, u32[]{:S(2)}) copy-start(f32[2048,128]{1,0:T(8,128)} %param.9) | copy-start | bytes 3145732
  19.8 6.1 %copy-start.7 = (s32[512,4]{0,1:T(4,128)S(1)}, s32[512,4]{0,1:T(4,128)}, u32[]{:S(2)}) copy-start(s32[512,4]{0,1:T(4,128)} %param.14) | copy-start | bytes 24580
  19.8 6.2 %copy-start.6 = (s32[16,512]{1,0:T(8,128)S(1)}, s32[16,512]{1,0:T(8,128)}, u32[]{:S(2)}) copy-start(s32[16,512]{1,0:T(8,128)} %param.15) | copy-start | bytes 98308
  19.8 21.9 %all-to-all-start = ((f32[8,256,128]{2,1,0:T(8,128)}), f32[8,256,128]{2,1,0:T(8,128)S(1)}, u32[]{:S(2)}, u32[]{:S(2)}) async-start(f32[8,256,128]{2,1,0:T(8,128)} %bitcast.20), calls=%async_computation | async-start | bytes 2097152 | tf_op jit(solution)/shard_map/all_to_all | solution.py:298
  25.8 64.9 %all-gather.2.cloned.1.call-start = ((), (), s32[]{:S(2)}) async-start(), calls=%async_computation.4 | async-start | bytes 1114112 | tf_op jit(solution)/shard_map/all_gather | solution.py:322
  41.7 5.5 %collective-permute-start = (f32[256,128]{1,0:T(8,128)S(1)}, f32[256,128]{1,0:T(8,128)S(1)}, u32[]{:S(2)}, u32[]{:S(2)}) collective-permute-start(f32[256,128]{1,0:T(8,128)S(1)} %residual.1.refs_0_), channel_id=1, source_target_pairs={{0,1},{1,0},{2,3},{3,2},{4,5},{5,4},{6,7},{7,6},{8,9},{9,8},{10,11... | collective-permute-start | bytes 393224 | tf_op jit(solution)/shard_map/ppermute | solution.py:306
  42.6 7.3 %collective-permute-start.1 = (f32[256,128]{1,0:T(8,128)S(1)}, f32[256,128]{1,0:T(8,128)S(1)}, u32[]{:S(2)}, u32[]{:S(2)}) collective-permute-start(f32[256,128]{1,0:T(8,128)S(1)} %residual.1.refs_0_), channel_id=1, source_target_pairs={{0,2},{1,3},{2,0},{3,1},{4,6},{5,7},{6,4},{7,5},{8,10},{9,11},{10,... | collective-permute-start | bytes 393224 | tf_op jit(solution)/shard_map/ppermute | solution.py:302
  43.1 8.9 %collective-permute-start.3 = (f32[256,128]{1,0:T(8,128)S(1)}, f32[256,128]{1,0:T(8,128)S(1)}, u32[]{:S(2)}, u32[]{:S(2)}) collective-permute-start(f32[256,128]{1,0:T(8,128)S(1)} %residual.1.refs_0_), channel_id=1, source_target_pairs={{0,4},{1,5},{2,6},{3,7},{4,0},{5,1},{6,2},{7,3},{8,12},{9,13},{10,... | collective-permute-start | bytes 393224 | tf_op jit(solution)/shard_map/ppermute | solution.py:302
  45.2 10.8 %collective-permute-start.5 = (f32[256,128]{1,0:T(8,128)S(1)}, f32[256,128]{1,0:T(8,128)S(1)}, u32[]{:S(2)}, u32[]{:S(2)}) collective-permute-start(f32[256,128]{1,0:T(8,128)S(1)} %residual.1.refs_0_), channel_id=1, source_target_pairs={{0,6},{1,7},{2,4},{3,5},{4,2},{5,3},{6,0},{7,1},{8,14},{9,15},{10,... | collective-permute-start | bytes 393224 | tf_op jit(solution)/shard_map/ppermute | solution.py:302
  47.3 8.7 %collective-permute-start.2 = (f32[256,128]{1,0:T(8,128)S(1)}, f32[256,128]{1,0:T(8,128)S(1)}, u32[]{:S(2)}, u32[]{:S(2)}) collective-permute-start(f32[256,128]{1,0:T(8,128)S(1)} %collective-permute-done.refs_1_), channel_id=1, source_target_pairs={{0,2},{1,3},{2,0},{3,1},{4,6},{5,7},{6,4},{7,5},{8,10},{9,11},{10,... | collective-permute-start | bytes 393224 | tf_op jit(solution)/shard_map/ppermute | solution.py:302
  47.6 8.4 %collective-permute-start.4 = (f32[256,128]{1,0:T(8,128)S(1)}, f32[256,128]{1,0:T(8,128)S(1)}, u32[]{:S(2)}, u32[]{:S(2)}) collective-permute-start(f32[256,128]{1,0:T(8,128)S(1)} %collective-permute-done.refs_1_), channel_id=1, source_target_pairs={{0,4},{1,5},{2,6},{3,7},{4,0},{5,1},{6,2},{7,3},{8,12},{9,13},{10,... | collective-permute-start | bytes 393224 | tf_op jit(solution)/shard_map/ppermute | solution.py:302
  49.9 7.9 %collective-permute-start.6 = (f32[256,128]{1,0:T(8,128)S(1)}, f32[256,128]{1,0:T(8,128)S(1)}, u32[]{:S(2)}, u32[]{:S(2)}) collective-permute-start(f32[256,128]{1,0:T(8,128)S(1)} %collective-permute-done.refs_1_), channel_id=1, source_target_pairs={{0,6},{1,7},{2,4},{3,5},{4,2},{5,3},{6,0},{7,1},{8,14},{9,15},{10,... | collective-permute-start | bytes 393224 | tf_op jit(solution)/shard_map/ppermute | solution.py:302
  57.8 1.6 copy-start.2
  61.3 35.5 %copy-start.1 = (f32[8,256,256]{2,1,0:T(8,128)S(1)}, f32[8,256,256]{2,1,0:T(8,128)}, u32[]{:S(2)}) copy-start(f32[8,256,256]{2,1,0:T(8,128)} %refs_10_.1) | copy-start | bytes 6291460
  61.3 35.5 %copy-start.5 = (f32[8,256]{1,0:T(8,128)S(1)}, f32[8,256]{1,0:T(8,128)}, u32[]{:S(2)}) copy-start(f32[8,256]{1,0:T(8,128)} %refs_11_.1) | copy-start | bytes 24580
  80.0 6.0 %collective-permute-start.7 = (f32[128,256]{1,0:T(8,128)S(1)}, f32[128,256]{1,0:T(8,128)S(1)}, u32[]{:S(2)}, u32[]{:S(2)}) collective-permute-start(f32[128,256]{1,0:T(8,128)S(1)} %separator.1.refs_0_), channel_id=1, source_target_pairs={{0,1},{1,0},{2,3},{3,2},{4,5},{5,4},{6,7},{7,6},{8,9},{9,8},{10,11... | collective-permute-start | bytes 393224 | tf_op jit(solution)/shard_map/ppermute | solution.py:306
  81.3 7.3 %collective-permute-start.8 = (f32[128,256]{1,0:T(8,128)S(1)}, f32[128,256]{1,0:T(8,128)S(1)}, u32[]{:S(2)}, u32[]{:S(2)}) collective-permute-start(f32[128,256]{1,0:T(8,128)S(1)} %separator.1.refs_0_), channel_id=1, source_target_pairs={{0,2},{1,3},{2,0},{3,1},{4,6},{5,7},{6,4},{7,5},{8,10},{9,11},{10,... | collective-permute-start | bytes 393224 | tf_op jit(solution)/shard_map/ppermute | solution.py:302
  81.9 9.9 %collective-permute-start.10 = (f32[128,256]{1,0:T(8,128)S(1)}, f32[128,256]{1,0:T(8,128)}, u32[]{:S(2)}, u32[]{:S(2)}) collective-permute-start(f32[128,256]{1,0:T(8,128)S(1)} %separator.1.refs_0_), channel_id=1, source_target_pairs={{0,4},{1,5},{2,6},{3,7},{4,0},{5,1},{6,2},{7,3},{8,12},{9,13},{10,... | collective-permute-start | bytes 393224 | tf_op jit(solution)/shard_map/ppermute | solution.py:302
  84.0 11.4 %collective-permute-start.12 = (f32[128,256]{1,0:T(8,128)S(1)}, f32[128,256]{1,0:T(8,128)}, u32[]{:S(2)}, u32[]{:S(2)}) collective-permute-start(f32[128,256]{1,0:T(8,128)S(1)} %separator.1.refs_0_), channel_id=1, source_target_pairs={{0,6},{1,7},{2,4},{3,5},{4,2},{5,3},{6,0},{7,1},{8,14},{9,15},{10,... | collective-permute-start | bytes 393224 | tf_op jit(solution)/shard_map/ppermute | solution.py:302
  86.0 9.3 %collective-permute-start.9 = (f32[128,256]{1,0:T(8,128)S(1)}, f32[128,256]{1,0:T(8,128)}, u32[]{:S(2)}, u32[]{:S(2)}) collective-permute-start(f32[128,256]{1,0:T(8,128)S(1)} %collective-permute-done.7.refs_1_), channel_id=1, source_target_pairs={{0,2},{1,3},{2,0},{3,1},{4,6},{5,7},{6,4},{7,5},{8,10},{9,11},{10,... | collective-permute-start | bytes 393224 | tf_op jit(solution)/shard_map/ppermute | solution.py:302
  86.0 9.3 %collective-permute-start.11 = (f32[128,256]{1,0:T(8,128)S(1)}, f32[128,256]{1,0:T(8,128)}, u32[]{:S(2)}, u32[]{:S(2)}) collective-permute-start(f32[128,256]{1,0:T(8,128)S(1)} %collective-permute-done.7.refs_1_), channel_id=1, source_target_pairs={{0,4},{1,5},{2,6},{3,7},{4,0},{5,1},{6,2},{7,3},{8,12},{9,13},{10,... | collective-permute-start | bytes 393224 | tf_op jit(solution)/shard_map/ppermute | solution.py:302
  88.7 8.1 %collective-permute-start.13 = (f32[128,256]{1,0:T(8,128)S(1)}, f32[128,256]{1,0:T(8,128)}, u32[]{:S(2)}, u32[]{:S(2)}) collective-permute-start(f32[128,256]{1,0:T(8,128)S(1)} %collective-permute-done.7.refs_1_), channel_id=1, source_target_pairs={{0,6},{1,7},{2,4},{3,5},{4,2},{5,3},{6,0},{7,1},{8,14},{9,15},{10,... | collective-permute-start | bytes 393224 | tf_op jit(solution)/shard_map/ppermute | solution.py:302
  96.8 1.2 copy-start.4
  110.1 29.0 %copy-start.3 = (f32[512,512]{1,0:T(8,128)S(1)}, f32[512,512]{1,0:T(8,128)}, u32[]{:S(2)}) copy-start(f32[512,512]{1,0:T(8,128)} %all-gather.2.cloned.1.call-done.lists_ref) | copy-start | bytes 3145732
  136.4 2.7 %collective-permute-start.14 = (f32[8,256,128]{2,1,0:T(8,128)S(1)}, f32[8,256,128]{2,1,0:T(8,128)S(1)}, u32[]{:S(2)}, u32[]{:S(2)}) collective-permute-start(f32[8,256,128]{2,1,0:T(8,128)S(1)} %bitcast.14), channel_id=1, source_target_pairs={{0,8},{8,0},{1,9},{9,1},{2,10},{10,2},{3,11},{11,3},{4,12},{12,4},... | collective-permute-start | bytes 3145736 | tf_op jit(solution)/shard_map/ppermute | solution.py:335
Sparse Core Ops, SparseCore 0:
  29.1 47.3 all-gather.1

commit v4 on v3

--- a/solution.py
+++ b/solution.py
@@ -6,7 +6,6 @@
 from jax.experimental.pallas import tpu as pltpu
 from jax.sharding import Mesh, PartitionSpec as P
 
-UNROLL = 64
 CHIPS = 64
 
 
@@ -208,23 +207,19 @@
     def field(at):
         return rows_ref[pl.ds(pl.multiple_of(el_ref[at], 2), 2), :]
 
-    def body(group, carry):
-        base = pl.multiple_of(group * UNROLL, UNROLL)
-        for step in range(UNROLL):
-            q = base + step
-            a = field(q)
-            b = field(quads_n + q)
-            c = field(2 * quads_n + q)
-            d = field(3 * quads_n + q)
-            prod_ref[pl.ds(2 * base + 2 * step, 2), :] = (a - b) * (c - d)
-        return carry
-
-    lax.fori_loop(0, quads_n // UNROLL, body, 0)
+    def load(q):
+        a = field(q)
+        b = field(quads_n + q)
+        c = field(2 * quads_n + q)
+        d = field(3 * quads_n + q)
+        prod_ref[2 * q : 2 * q + 2, :] = (a - b) * (c - d)
 
     lane = lax.broadcasted_iota(jnp.int32, (128, 128), 1)
     second = lane & 8 != 0
     upper = lane & 4 != 0
     for pair in range(2):
+        for q in range(pair * 256, pair * 256 + 256):
+            load(q)
         for t2 in range(2):
             at = (pair * 2 + t2) * 128
             lanes_ref[...] = lists_ref[:16, at : at + 128].astype(jnp.int32) * 2

time: 192 us -> 189 us (0.984)
  Pallas kernels: 48.6 us -> 46 us
    pallas_call x1, Pallas kernels: 19.4 us -> 16.8 us  [select(): pl.pallas_call(select_kernel, grid_spec=pltpu.PrefetchScalarGridSpec(num_...]
where the time goes in v4:
time: 189 us; the launch traced here: 188 us
  blocking collectives  68.6 us (36%)
  Pallas kernels  46 us (24%)
  waiting for transfers between devices  28.4 us (15%)
  starting transfers between devices  27 us (14%)
  between operations  13.5 us (7%)
  local copies, waits for them, and re-layouts  2.96 us (2%)
    all_to_all x1, blocking collectives, local(): lax.all_to_all(fields.reshape(CHIPS, 32, 128), ('chip', 'y', 'z'), 0, 0,...  26.3 us
    all_to_all x1, blocking collectives, local(): received = lax.all_to_all(picked, ('chip', 'y', 'z'), 0, 0, tiled=True)  23.7 us
    ppermute x12, starting transfers between devices, send(): return lax.ppermute(value, ('y', 'z'), [(i, i ^ d) for i in range(8)])  18.8 us
    all_to_all x1, blocking collectives, exchange(): return lax.all_to_all(parts, ('y', 'z'), 0, 0, tiled=True)  18.7 us
    pallas_call x1, Pallas kernels, select(): pl.pallas_call(select_kernel, grid_spec=pltpu.PrefetchScalarGridSpec(num_...  16.8 us
    all_to_all x1, waiting for transfers between devices, exchange(): return lax.all_to_all(parts, ('y', 'z'), 0, 0, tiled=True)  14.9 us
    pallas_call x1, Pallas kernels, front(): pl.pallas_call(front_kernel, grid=(8,), out_shape=(jax.ShapeDtypeStruct((...  13.2 us
    pallas_call x1, Pallas kernels, back(): pl.pallas_call(back_kernel, grid_spec=pltpu.PrefetchScalarGridSpec(num_sc...  12.1 us
  transfers between devices with their start and end apart: 17, of which 6 were waited for; matrix products, arithmetic and copies ran while one was open for 1% of the time, Pallas kernels for 1%

profile of v4, /device:TPU:0, one launch (start us, length us, event | category | flops | bytes accessed | tf_op | source)
XLA Modules:
  0.0 188.3 jit_solution(3065948252882760501)
XLA Ops:
  6.5 13.2 %leaf_front.1 = (f32[2048,128]{1,0:T(8,128)}, f32[8,128,256]{2,1,0:T(8,128)}) custom-call(f32[8,256,256]{2,1,0:T(8,128)} %refs_10_.1, f32[8,256,128]{2,1,0:T(8,128)} %rhs_ref.1, f32[8,2048,256]{2,1,0:T(8,128)} %refs_9_.1), custom_call_target="tpu_custom_call" | custom-call | tf_op jit(solution)/shard_map/leaf_front/pallas_call | solution.py:51
  19.8 6.1 %all-to-all-start = ((f32[8,256,128]{2,1,0:T(8,128)}), f32[8,256,128]{2,1,0:T(8,128)S(1)}, u32[]{:S(2)}, u32[]{:S(2)}) async-start(f32[8,256,128]{2,1,0:T(8,128)} %bitcast.20), calls=%async_computation | async-start | bytes 2097152 | tf_op jit(solution)/shard_map/all_to_all | solution.py:293
  26.0 0.7 add_convert_fusion
  26.7 14.9 %all-to-all-done.parts_ref = f32[8,256,128]{2,1,0:T(8,128)S(1)} async-done(((f32[8,256,128]{2,1,0:T(8,128)}), f32[8,256,128]{2,1,0:T(8,128)S(1)}, u32[]{:S(2)}, u32[]{:S(2)}) %all-to-all-start) | async-done | bytes 1048608 | tf_op jit(solution)/shard_map/all_to_all | solution.py:293
  41.7 0.8 collective-permute-start
  42.6 0.6 collective-permute-start.1
  43.1 2.1 %collective-permute-start.3 = (f32[256,128]{1,0:T(8,128)S(1)}, f32[256,128]{1,0:T(8,128)S(1)}, u32[]{:S(2)}, u32[]{:S(2)}) collective-permute-start(f32[256,128]{1,0:T(8,128)S(1)} %residual.1.refs_0_), channel_id=1, source_target_pairs={{0,4},{1,5},{2,6},{3,7},{4,0},{5,1},{6,2},{7,3},{8,12},{9,13},{10,... | collective-permute-start | bytes 393224 | tf_op jit(solution)/shard_map/ppermute | solution.py:297
  45.2 2.1 %collective-permute-start.5 = (f32[256,128]{1,0:T(8,128)S(1)}, f32[256,128]{1,0:T(8,128)S(1)}, u32[]{:S(2)}, u32[]{:S(2)}) collective-permute-start(f32[256,128]{1,0:T(8,128)S(1)} %residual.1.refs_0_), channel_id=1, source_target_pairs={{0,6},{1,7},{2,4},{3,5},{4,2},{5,3},{6,0},{7,1},{8,14},{9,15},{10,... | collective-permute-start | bytes 393224 | tf_op jit(solution)/shard_map/ppermute | solution.py:297
  47.3 0.4 collective-permute-start.2
  47.6 2.3 %collective-permute-start.4 = (f32[256,128]{1,0:T(8,128)S(1)}, f32[256,128]{1,0:T(8,128)S(1)}, u32[]{:S(2)}, u32[]{:S(2)}) collective-permute-start(f32[256,128]{1,0:T(8,128)S(1)} %collective-permute-done.refs_1_), channel_id=1, source_target_pairs={{0,4},{1,5},{2,6},{3,7},{4,0},{5,1},{6,2},{7,3},{8,12},{9,13},{10,... | collective-permute-start | bytes 393224 | tf_op jit(solution)/shard_map/ppermute | solution.py:297
  49.9 2.1 %collective-permute-start.6 = (f32[256,128]{1,0:T(8,128)S(1)}, f32[256,128]{1,0:T(8,128)S(1)}, u32[]{:S(2)}, u32[]{:S(2)}) collective-permute-start(f32[256,128]{1,0:T(8,128)S(1)} %collective-permute-done.refs_1_), channel_id=1, source_target_pairs={{0,6},{1,7},{2,4},{3,5},{4,2},{5,3},{6,0},{7,1},{8,14},{9,15},{10,... | collective-permute-start | bytes 393224 | tf_op jit(solution)/shard_map/ppermute | solution.py:297
  52.0 3.9 %collective-permute-done.5.refs_6_ = f32[256,128]{1,0:T(8,128)S(1)} collective-permute-done((f32[256,128]{1,0:T(8,128)S(1)}, f32[256,128]{1,0:T(8,128)S(1)}, u32[]{:S(2)}, u32[]{:S(2)}) %collective-permute-start.5) | collective-permute-done | bytes 131104 | tf_op jit(solution)/shard_map/ppermute | solution.py:297
  56.0 1.8 collective-permute-done.6.refs_7_
  57.8 1.6 copy-done.2
  59.4 1.9 top_solve.1
  61.3 18.7 %all_to_all.20.parts_ref = f32[8,128,256]{2,1,0:T(8,128)S(1)} all-to-all(f32[8,128,256]{2,1,0:T(8,128)S(1)} %top_solve.1), channel_id=1, replica_groups=mesh['chip'=8,'core'=2,'y'=4,'z'=2] {'y','z'}, dimensions={0} | all-to-all | bytes 2097152 | tf_op jit(solution)/shard_map/all_to_all | solution.py:293
  80.1 1.3 collective-permute-start.7
  81.3 0.6 collective-permute-start.8
  81.9 2.1 %collective-permute-start.10 = (f32[128,256]{1,0:T(8,128)S(1)}, f32[128,256]{1,0:T(8,128)}, u32[]{:S(2)}, u32[]{:S(2)}) collective-permute-start(f32[128,256]{1,0:T(8,128)S(1)} %separator.1.refs_0_), channel_id=1, source_target_pairs={{0,4},{1,5},{2,6},{3,7},{4,0},{5,1},{6,2},{7,3},{8,12},{9,13},{10,... | collective-permute-start | bytes 393224 | tf_op jit(solution)/shard_map/ppermute | solution.py:297
  84.0 2.1 %collective-permute-start.12 = (f32[128,256]{1,0:T(8,128)S(1)}, f32[128,256]{1,0:T(8,128)}, u32[]{:S(2)}, u32[]{:S(2)}) collective-permute-start(f32[128,256]{1,0:T(8,128)S(1)} %separator.1.refs_0_), channel_id=1, source_target_pairs={{0,6},{1,7},{2,4},{3,5},{4,2},{5,3},{6,0},{7,1},{8,14},{9,15},{10,... | collective-permute-start | bytes 393224 | tf_op jit(solution)/shard_map/ppermute | solution.py:297
  86.0 2.6 %collective-permute-start.11 = (f32[128,256]{1,0:T(8,128)S(1)}, f32[128,256]{1,0:T(8,128)}, u32[]{:S(2)}, u32[]{:S(2)}) collective-permute-start(f32[128,256]{1,0:T(8,128)S(1)} %collective-permute-done.7.refs_1_), channel_id=1, source_target_pairs={{0,4},{1,5},{2,6},{3,7},{4,0},{5,1},{6,2},{7,3},{8,12},{9,13},{10,... | collective-permute-start | bytes 393224 | tf_op jit(solution)/shard_map/ppermute | solution.py:297
  88.7 2.1 %collective-permute-start.13 = (f32[128,256]{1,0:T(8,128)S(1)}, f32[128,256]{1,0:T(8,128)}, u32[]{:S(2)}, u32[]{:S(2)}) collective-permute-start(f32[128,256]{1,0:T(8,128)S(1)} %collective-permute-done.7.refs_1_), channel_id=1, source_target_pairs={{0,6},{1,7},{2,4},{3,5},{4,2},{5,3},{6,0},{7,1},{8,14},{9,15},{10,... | collective-permute-start | bytes 393224 | tf_op jit(solution)/shard_map/ppermute | solution.py:297
  90.7 1.0 fusion.1
  91.8 3.6 %collective-permute-done.12.refs_6_ = f32[128,256]{1,0:T(8,128)} collective-permute-done((f32[128,256]{1,0:T(8,128)S(1)}, f32[128,256]{1,0:T(8,128)}, u32[]{:S(2)}, u32[]{:S(2)}) %collective-permute-start.12) | collective-permute-done | bytes 131104 | tf_op jit(solution)/shard_map/ppermute | solution.py:297
  95.4 1.4 collective-permute-done.13.refs_7_
  96.8 1.2 copy-done.4
  98.0 12.1 %leaf_back.1 = f32[2048,128]{1,0:T(8,128)S(1)} custom-call(s32[2]{0:T(128)S(1)} %pad_add_fusion.me_ref, f32[128,256]{1,0:T(8,128)S(1)} %separator.1.refs_0_, f32[128,256]{1,0:T(8,128)S(1)} %collective-permute-done.7.refs_1_, f32[128,256]{1,0:T(8,128)S(1)} %collective-permute-done.8.refs_2_, f32[128,256]{1,0:T(8,128)} %collective-permute-done.9.refs_3_, ...), custom_call_target="tpu_custom_call" | custom-call | tf_op jit(solution)/shard_map/leaf_back/pallas_call | solution.py:171
  110.2 26.3 %all_to_all.21 = f32[64,32,128]{2,1,0:T(8,128)S(1)} all-to-all(f32[64,32,128]{2,1,0:T(8,128)S(1)} %bitcast.16), channel_id=1, replica_groups=mesh['chip'=8,'core'=2,'y'=4,'z'=2] {'chip','y','z'}, dimensions={0} | all-to-all | bytes 2097152 | tf_op jit(solution)/shard_map/all_to_all | solution.py:328
  136.4 2.7 %collective-permute-done.14.other_ref = f32[8,256,128]{2,1,0:T(8,128)S(1)} collective-permute-done((f32[8,256,128]{2,1,0:T(8,128)S(1)}, f32[8,256,128]{2,1,0:T(8,128)S(1)}, u32[]{:S(2)}, u32[]{:S(2)}) %collective-permute-start.14) | collective-permute-done | bytes 1048608 | tf_op jit(solution)/shard_map/ppermute | solution.py:330
  139.1 16.8 %select_quads.1 = f32[64,32,128]{2,1,0:T(8,128)S(1)} custom-call(s32[1]{0:T(128)} %bitcast.core_ref, s32[16384]{0:T(1024)S(1)} %bitcast.19, f32[512,512]{1,0:T(8,128)S(1)} %copy-done.3, f32[8,256,128]{2,1,0:T(8,128)S(1)} %bitcast.15, f32[8,256,128]{2,1,0:T(8,128)S(1)} %collective-permute-done.14.other_ref), custom_call_target="tpu_custom_call" | custom-call | tf_op jit(solution)/shard_map/select_quads/pallas_call | solution.py:245
  155.9 23.7 %all_to_all.22 = f32[64,32,128]{2,1,0:T(8,128)S(1)} all-to-all(f32[64,32,128]{2,1,0:T(8,128)S(1)} %select_quads.1), channel_id=1, replica_groups=mesh['chip'=8,'core'=2,'y'=4,'z'=2] {'chip','y','z'}, dimensions={0} | all-to-all | bytes 2097152 | tf_op jit(solution)/shard_map/all_to_all | solution.py:332
  179.5 1.9 %assemble_sens.1 = f32[2,4,64,512]{3,2,1,0:T(8,128)} custom-call(f32[2048,128]{1,0:T(8,128)S(1)} %bitcast.17), custom_call_target="tpu_custom_call" | custom-call | tf_op jit(solution)/shard_map/assemble_sens/pallas_call | solution.py:281
  (37 shorter events, 0.4 us)
Async XLA Ops:
  6.5 20.2 %copy-start = (f32[2048,128]{1,0:T(8,128)S(1)}, f32[2048,128]{1,0:T(8,128)}, u32[]{:S(2)}) copy-start(f32[2048,128]{1,0:T(8,128)} %param.9) | copy-start | bytes 3145732
  19.8 6.1 %copy-start.7 = (s32[512,4]{0,1:T(4,128)S(1)}, s32[512,4]{0,1:T(4,128)}, u32[]{:S(2)}) copy-start(s32[512,4]{0,1:T(4,128)} %param.14) | copy-start | bytes 24580
  19.8 6.2 %copy-start.6 = (s32[16,512]{1,0:T(8,128)S(1)}, s32[16,512]{1,0:T(8,128)}, u32[]{:S(2)}) copy-start(s32[16,512]{1,0:T(8,128)} %param.15) | copy-start | bytes 98308
  19.8 21.9 %all-to-all-start = ((f32[8,256,128]{2,1,0:T(8,128)}), f32[8,256,128]{2,1,0:T(8,128)S(1)}, u32[]{:S(2)}, u32[]{:S(2)}) async-start(f32[8,256,128]{2,1,0:T(8,128)} %bitcast.20), calls=%async_computation | async-start | bytes 2097152 | tf_op jit(solution)/shard_map/all_to_all | solution.py:293
  25.8 64.9 %all-gather.2.cloned.1.call-start = ((), (), s32[]{:S(2)}) async-start(), calls=%async_computation.4 | async-start | bytes 1114112 | tf_op jit(solution)/shard_map/all_gather | solution.py:317
  41.7 5.5 %collective-permute-start = (f32[256,128]{1,0:T(8,128)S(1)}, f32[256,128]{1,0:T(8,128)S(1)}, u32[]{:S(2)}, u32[]{:S(2)}) collective-permute-start(f32[256,128]{1,0:T(8,128)S(1)} %residual.1.refs_0_), channel_id=1, source_target_pairs={{0,1},{1,0},{2,3},{3,2},{4,5},{5,4},{6,7},{7,6},{8,9},{9,8},{10,11... | collective-permute-start | bytes 393224 | tf_op jit(solution)/shard_map/ppermute | solution.py:301
  42.6 7.3 %collective-permute-start.1 = (f32[256,128]{1,0:T(8,128)S(1)}, f32[256,128]{1,0:T(8,128)S(1)}, u32[]{:S(2)}, u32[]{:S(2)}) collective-permute-start(f32[256,128]{1,0:T(8,128)S(1)} %residual.1.refs_0_), channel_id=1, source_target_pairs={{0,2},{1,3},{2,0},{3,1},{4,6},{5,7},{6,4},{7,5},{8,10},{9,11},{10,... | collective-permute-start | bytes 393224 | tf_op jit(solution)/shard_map/ppermute | solution.py:297
  43.1 8.9 %collective-permute-start.3 = (f32[256,128]{1,0:T(8,128)S(1)}, f32[256,128]{1,0:T(8,128)S(1)}, u32[]{:S(2)}, u32[]{:S(2)}) collective-permute-start(f32[256,128]{1,0:T(8,128)S(1)} %residual.1.refs_0_), channel_id=1, source_target_pairs={{0,4},{1,5},{2,6},{3,7},{4,0},{5,1},{6,2},{7,3},{8,12},{9,13},{10,... | collective-permute-start | bytes 393224 | tf_op jit(solution)/shard_map/ppermute | solution.py:297
  45.2 10.8 %collective-permute-start.5 = (f32[256,128]{1,0:T(8,128)S(1)}, f32[256,128]{1,0:T(8,128)S(1)}, u32[]{:S(2)}, u32[]{:S(2)}) collective-permute-start(f32[256,128]{1,0:T(8,128)S(1)} %residual.1.refs_0_), channel_id=1, source_target_pairs={{0,6},{1,7},{2,4},{3,5},{4,2},{5,3},{6,0},{7,1},{8,14},{9,15},{10,... | collective-permute-start | bytes 393224 | tf_op jit(solution)/shard_map/ppermute | solution.py:297
  47.3 8.7 %collective-permute-start.2 = (f32[256,128]{1,0:T(8,128)S(1)}, f32[256,128]{1,0:T(8,128)S(1)}, u32[]{:S(2)}, u32[]{:S(2)}) collective-permute-start(f32[256,128]{1,0:T(8,128)S(1)} %collective-permute-done.refs_1_), channel_id=1, source_target_pairs={{0,2},{1,3},{2,0},{3,1},{4,6},{5,7},{6,4},{7,5},{8,10},{9,11},{10,... | collective-permute-start | bytes 393224 | tf_op jit(solution)/shard_map/ppermute | solution.py:297
  47.6 8.4 %collective-permute-start.4 = (f32[256,128]{1,0:T(8,128)S(1)}, f32[256,128]{1,0:T(8,128)S(1)}, u32[]{:S(2)}, u32[]{:S(2)}) collective-permute-start(f32[256,128]{1,0:T(8,128)S(1)} %collective-permute-done.refs_1_), channel_id=1, source_target_pairs={{0,4},{1,5},{2,6},{3,7},{4,0},{5,1},{6,2},{7,3},{8,12},{9,13},{10,... | collective-permute-start | bytes 393224 | tf_op jit(solution)/shard_map/ppermute | solution.py:297
  49.9 7.9 %collective-permute-start.6 = (f32[256,128]{1,0:T(8,128)S(1)}, f32[256,128]{1,0:T(8,128)S(1)}, u32[]{:S(2)}, u32[]{:S(2)}) collective-permute-start(f32[256,128]{1,0:T(8,128)S(1)} %collective-permute-done.refs_1_), channel_id=1, source_target_pairs={{0,6},{1,7},{2,4},{3,5},{4,2},{5,3},{6,0},{7,1},{8,14},{9,15},{10,... | collective-permute-start | bytes 393224 | tf_op jit(solution)/shard_map/ppermute | solution.py:297
  57.8 1.6 copy-start.2
  61.3 35.5 %copy-start.1 = (f32[8,256,256]{2,1,0:T(8,128)S(1)}, f32[8,256,256]{2,1,0:T(8,128)}, u32[]{:S(2)}) copy-start(f32[8,256,256]{2,1,0:T(8,128)} %refs_10_.1) | copy-start | bytes 6291460
  61.3 35.5 %copy-start.5 = (f32[8,256]{1,0:T(8,128)S(1)}, f32[8,256]{1,0:T(8,128)}, u32[]{:S(2)}) copy-start(f32[8,256]{1,0:T(8,128)} %refs_11_.1) | copy-start | bytes 24580
  80.1 6.0 %collective-permute-start.7 = (f32[128,256]{1,0:T(8,128)S(1)}, f32[128,256]{1,0:T(8,128)S(1)}, u32[]{:S(2)}, u32[]{:S(2)}) collective-permute-start(f32[128,256]{1,0:T(8,128)S(1)} %separator.1.refs_0_), channel_id=1, source_target_pairs={{0,1},{1,0},{2,3},{3,2},{4,5},{5,4},{6,7},{7,6},{8,9},{9,8},{10,11... | collective-permute-start | bytes 393224 | tf_op jit(solution)/shard_map/ppermute | solution.py:301
  81.3 7.3 %collective-permute-start.8 = (f32[128,256]{1,0:T(8,128)S(1)}, f32[128,256]{1,0:T(8,128)S(1)}, u32[]{:S(2)}, u32[]{:S(2)}) collective-permute-start(f32[128,256]{1,0:T(8,128)S(1)} %separator.1.refs_0_), channel_id=1, source_target_pairs={{0,2},{1,3},{2,0},{3,1},{4,6},{5,7},{6,4},{7,5},{8,10},{9,11},{10,... | collective-permute-start | bytes 393224 | tf_op jit(solution)/shard_map/ppermute | solution.py:297
  81.9 9.9 %collective-permute-start.10 = (f32[128,256]{1,0:T(8,128)S(1)}, f32[128,256]{1,0:T(8,128)}, u32[]{:S(2)}, u32[]{:S(2)}) collective-permute-start(f32[128,256]{1,0:T(8,128)S(1)} %separator.1.refs_0_), channel_id=1, source_target_pairs={{0,4},{1,5},{2,6},{3,7},{4,0},{5,1},{6,2},{7,3},{8,12},{9,13},{10,... | collective-permute-start | bytes 393224 | tf_op jit(solution)/shard_map/ppermute | solution.py:297
  84.0 11.4 %collective-permute-start.12 = (f32[128,256]{1,0:T(8,128)S(1)}, f32[128,256]{1,0:T(8,128)}, u32[]{:S(2)}, u32[]{:S(2)}) collective-permute-start(f32[128,256]{1,0:T(8,128)S(1)} %separator.1.refs_0_), channel_id=1, source_target_pairs={{0,6},{1,7},{2,4},{3,5},{4,2},{5,3},{6,0},{7,1},{8,14},{9,15},{10,... | collective-permute-start | bytes 393224 | tf_op jit(solution)/shard_map/ppermute | solution.py:297
  86.0 9.3 %collective-permute-start.9 = (f32[128,256]{1,0:T(8,128)S(1)}, f32[128,256]{1,0:T(8,128)}, u32[]{:S(2)}, u32[]{:S(2)}) collective-permute-start(f32[128,256]{1,0:T(8,128)S(1)} %collective-permute-done.7.refs_1_), channel_id=1, source_target_pairs={{0,2},{1,3},{2,0},{3,1},{4,6},{5,7},{6,4},{7,5},{8,10},{9,11},{10,... | collective-permute-start | bytes 393224 | tf_op jit(solution)/shard_map/ppermute | solution.py:297
  86.0 9.3 %collective-permute-start.11 = (f32[128,256]{1,0:T(8,128)S(1)}, f32[128,256]{1,0:T(8,128)}, u32[]{:S(2)}, u32[]{:S(2)}) collective-permute-start(f32[128,256]{1,0:T(8,128)S(1)} %collective-permute-done.7.refs_1_), channel_id=1, source_target_pairs={{0,4},{1,5},{2,6},{3,7},{4,0},{5,1},{6,2},{7,3},{8,12},{9,13},{10,... | collective-permute-start | bytes 393224 | tf_op jit(solution)/shard_map/ppermute | solution.py:297
  88.7 8.1 %collective-permute-start.13 = (f32[128,256]{1,0:T(8,128)S(1)}, f32[128,256]{1,0:T(8,128)}, u32[]{:S(2)}, u32[]{:S(2)}) collective-permute-start(f32[128,256]{1,0:T(8,128)S(1)} %collective-permute-done.7.refs_1_), channel_id=1, source_target_pairs={{0,6},{1,7},{2,4},{3,5},{4,2},{5,3},{6,0},{7,1},{8,14},{9,15},{10,... | collective-permute-start | bytes 393224 | tf_op jit(solution)/shard_map/ppermute | solution.py:297
  96.8 1.2 copy-start.4
  110.1 28.9 %copy-start.3 = (f32[512,512]{1,0:T(8,128)S(1)}, f32[512,512]{1,0:T(8,128)}, u32[]{:S(2)}) copy-start(f32[512,512]{1,0:T(8,128)} %all-gather.2.cloned.1.call-done.lists_ref) | copy-start | bytes 3145732
  136.4 2.7 %collective-permute-start.14 = (f32[8,256,128]{2,1,0:T(8,128)S(1)}, f32[8,256,128]{2,1,0:T(8,128)S(1)}, u32[]{:S(2)}, u32[]{:S(2)}) collective-permute-start(f32[8,256,128]{2,1,0:T(8,128)S(1)} %bitcast.14), channel_id=1, source_target_pairs={{0,8},{8,0},{1,9},{9,1},{2,10},{10,2},{3,11},{11,3},{4,12},{12,4},... | collective-permute-start | bytes 3145736 | tf_op jit(solution)/shard_map/ppermute | solution.py:330
Sparse Core Ops, SparseCore 0:
  29.1 47.3 all-gather.1

commit v5 on v4

--- a/solution.py
+++ b/solution.py
@@ -135,21 +135,61 @@
     )(me, inv, *res)
 
 
+def store_split(me_ref, sep, split_ref):
+    for d, ref in enumerate(sep):
+        cols = pl.ds(pl.multiple_of((d // 2) * 512 + (me_ref[1] ^ (d % 2)) * 256, 256), 256)
+        split_ref[:128, cols], split_ref[128:, cols] = two(ref[...])
+
+
+def minus_terms(total, split_ref, coupling_refs):
+    for n, ref in enumerate(coupling_refs):
+        cols = slice(n * 512, n * 512 + 512)
+        ch, cl = two(ref[0])
+        wide = mm(split_ref[:, cols], ch)
+        total = total - (wide[:128] + wide[128:] + mm(split_ref[:128, cols], cl))
+    return total
+
+
+def near_kernel(me_ref, own_ref, far_ref, forward_ref, coupling_ref, out_ref, split_ref):
+    @pl.when(pl.program_id(0) == 0)
+    def _():
+        store_split(me_ref, (own_ref, far_ref), split_ref)
+
+    out_ref[0] = minus_terms(forward_ref[0], split_ref, (coupling_ref,))
+
+
+def panels(dy):
+    return pl.BlockSpec((1, 512, 256), lambda j, me: (j, me[0] ^ dy, 0))
+
+
+def near(me, sep, forward, coupling):
+    return pl.pallas_call(
+        near_kernel,
+        grid_spec=pltpu.PrefetchScalarGridSpec(
+            num_scalar_prefetch=1,
+            grid=(8,),
+            in_specs=[pl.BlockSpec((128, 256), lambda j, me: (0, 0))] * 2
+            + [pl.BlockSpec((1, 128, 256), lambda j, me: (j, 0, 0)), panels(0)],
+            out_specs=pl.BlockSpec((1, 128, 256), lambda j, me: (j, 0, 0)),
+            scratch_shapes=[pltpu.VMEM((256, 512), jnp.bfloat16)],
+        ),
+        out_shape=jax.ShapeDtypeStruct((8, 128, 256), jnp.float32),
+        compiler_params=params(48),
+        cost_estimate=pl.CostEstimate(flops=1_000_000_000, bytes_accessed=6_000_000, transcendentals=0),
+        name="leaf_near",
+    )(me, *sep, forward, coupling)
+
+
 def back_kernel(me_ref, *refs):
-    sep, (forward_ref, coupling_ref, inv_ref, cond_ref, out_ref, split_ref, total_ref) = refs[:8], refs[8:]
+    sep, forward_ref, coupling_refs, (inv_ref, cond_ref, out_ref, split_ref, total_ref) = (
+        refs[:6], refs[6], refs[7:10], refs[10:])
     j = pl.program_id(0)
 
     @pl.when(j == 0)
     def _():
-        for d in range(8):
-            p = (me_ref[0] ^ (d // 2)) * 2 + (me_ref[1] ^ (d % 2))
-            split_ref[p, :128], split_ref[p, 128:] = two(sep[d][...])
-
-    total = forward_ref[0]
-    for p in range(8):
-        ch, cl = two(coupling_ref[0, p * 256 : (p + 1) * 256, :])
-        wide = mm(split_ref[p], ch)
-        total = total - (wide[:128] + wide[128:] + mm(split_ref[p, :128], cl))
+        store_split(me_ref, sep, split_ref)
+
+    total = minus_terms(forward_ref[0], split_ref, coupling_refs)
     total_ref[j] = total
 
     @pl.when(j == 7)
@@ -173,23 +213,25 @@
         grid_spec=pltpu.PrefetchScalarGridSpec(
             num_scalar_prefetch=1,
             grid=(8,),
-            in_specs=[pl.BlockSpec((128, 256), lambda j, me: (0, 0))] * 8
+            in_specs=[pl.BlockSpec((128, 256), lambda j, me: (0, 0))] * 6
             + [
                 pl.BlockSpec((1, 128, 256), lambda j, me: (j, 0, 0)),
-                pl.BlockSpec((1, 2048, 256), lambda j, me: (j, 0, 0)),
+                panels(1),
+                panels(2),
+                panels(3),
                 pl.BlockSpec((8, 256, 256), lambda j, me: (0, 0, 0)),
                 pl.BlockSpec((8, 256), lambda j, me: (0, 0)),
             ],
             out_specs=pl.BlockSpec((CHIPS * 32, 128), lambda j, me: (0, 0)),
             scratch_shapes=[
-                pltpu.VMEM((8, 256, 256), jnp.bfloat16),
+                pltpu.VMEM((256, 1536), jnp.bfloat16),
                 pltpu.VMEM((8, 128, 256), jnp.float32),
             ],
         ),
         out_shape=jax.ShapeDtypeStruct((CHIPS * 32, 128), jnp.float32),
         compiler_params=params(48),
         name="leaf_back",
-    )(me, *sep, forward, coupling, inv, cond)
+    )(me, *sep, forward, coupling, coupling, coupling, inv, cond)
 
 
 def select_kernel(core_ref, el_ref, lists_ref, own_ref, other_ref, out_ref, rows_ref, prod_ref, ids_ref, lanes_ref):
@@ -322,9 +364,10 @@
     top_own = lax.dynamic_slice_in_dim(top_rhs, at, 256, 0)
     res = residual(top_own, exchange(partial_value.reshape(8, 256, 128)))
     separator = all_panels(total(exchange(top(me, top_inv, all_panels(res)))))
+    started = near(me, separator[:2], forward, coupling)
     separator, el, lists = lax.optimization_barrier((separator, el, lists))
 
-    fields = back(me, separator, forward, coupling, leaf_inv, cond)
+    fields = back(me, separator[2:], started, coupling, leaf_inv, cond)
     own = lax.all_to_all(fields.reshape(CHIPS, 32, 128), ("chip", "y", "z"), 0, 0, tiled=True)
     own = own.reshape(8, 256, 128)
     other = lax.ppermute(own, "core", [(0, 1), (1, 0)])

time: 189 us -> 184 us (0.974)
  Pallas kernels: 46 us -> 50.7 us
  waiting for transfers between devices: 28.4 us -> 23.7 us
  blocking collectives: 68.6 us -> 66.3 us
    pallas_call x0 -> x1, Pallas kernels: none -> 6.44 us  [near(): pl.pallas_call(near_kernel, grid_spec=pltpu.PrefetchScalarGridSpec(num_sc...]
    ppermute x12, waiting for transfers between devices: 10.8 us -> 5.81 us  [send(): return lax.ppermute(value, ('y', 'z'), [(i, i ^ d) for i in range(8)])]
    all_to_all x1, blocking collectives: 26.3 us -> 24.1 us  [local(): lax.all_to_all(fields.reshape(CHIPS, 32, 128), ('chip', 'y', 'z'), 0, 0,...]
  transfers between devices with their start and end apart: 17 -> 17, of which waited for: 6 -> 5; matrix products, arithmetic and copies ran while one was open for 1% -> 1% of each run, Pallas kernels for 1% -> 5%
where the time goes in v5:
time: 184 us; the launch traced here: 183 us
  blocking collectives  66.3 us (36%)
  Pallas kernels  50.7 us (28%)
  starting transfers between devices  25.3 us (14%)
  waiting for transfers between devices  23.7 us (13%)
  between operations  13.6 us (7%)
    all_to_all x1, blocking collectives, local(): lax.all_to_all(fields.reshape(CHIPS, 32, 128), ('chip', 'y', 'z'), 0, 0,...  24.1 us
    all_to_all x1, blocking collectives, local(): received = lax.all_to_all(picked, ('chip', 'y', 'z'), 0, 0, tiled=True)  23.5 us
    all_to_all x1, blocking collectives, exchange(): return lax.all_to_all(parts, ('y', 'z'), 0, 0, tiled=True)  18.7 us
    ppermute x12, starting transfers between devices, send(): return lax.ppermute(value, ('y', 'z'), [(i, i ^ d) for i in range(8)])  17.1 us
    pallas_call x1, Pallas kernels, select(): pl.pallas_call(select_kernel, grid_spec=pltpu.PrefetchScalarGridSpec(num_...  16.7 us
    all_to_all x1, waiting for transfers between devices, exchange(): return lax.all_to_all(parts, ('y', 'z'), 0, 0, tiled=True)  14.9 us
    pallas_call x1, Pallas kernels, front(): pl.pallas_call(front_kernel, grid=(8,), out_shape=(jax.ShapeDtypeStruct((...  13.2 us
    pallas_call x1, Pallas kernels, back(): pl.pallas_call(back_kernel, grid_spec=pltpu.PrefetchScalarGridSpec(num_sc...  10.4 us
  transfers between devices with their start and end apart: 17, of which 5 were waited for; matrix products, arithmetic and copies ran while one was open for 1% of the time, Pallas kernels for 5%

profile of v5, /device:TPU:0, one launch (start us, length us, event | category | flops | bytes accessed | tf_op | source)
XLA Modules:
  0.0 183.0 jit_solution(11903033372470064575)
XLA Ops:
  6.5 13.2 %leaf_front.1 = (f32[2048,128]{1,0:T(8,128)}, f32[8,128,256]{2,1,0:T(8,128)}) custom-call(f32[8,256,256]{2,1,0:T(8,128)} %refs_10_.1, f32[8,256,128]{2,1,0:T(8,128)} %rhs_ref.1, f32[8,2048,256]{2,1,0:T(8,128)} %refs_9_.1), custom_call_target="tpu_custom_call" | custom-call | tf_op jit(solution)/shard_map/leaf_front/pallas_call | solution.py:51
  19.8 6.1 %all-to-all-start = ((f32[8,256,128]{2,1,0:T(8,128)}), f32[8,256,128]{2,1,0:T(8,128)S(1)}, u32[]{:S(2)}, u32[]{:S(2)}) async-start(f32[8,256,128]{2,1,0:T(8,128)} %bitcast.20), calls=%async_computation | async-start | bytes 2097152 | tf_op jit(solution)/shard_map/all_to_all | solution.py:335
  25.9 0.1 pad.2.clone
  26.0 0.7 add_convert_fusion
  26.7 14.9 %all-to-all-done.parts_ref = f32[8,256,128]{2,1,0:T(8,128)S(1)} async-done(((f32[8,256,128]{2,1,0:T(8,128)}), f32[8,256,128]{2,1,0:T(8,128)S(1)}, u32[]{:S(2)}, u32[]{:S(2)}) %all-to-all-start) | async-done | bytes 1048608 | tf_op jit(solution)/shard_map/all_to_all | solution.py:335
  41.7 0.8 collective-permute-start
  42.6 0.6 collective-permute-start.1
  43.1 2.1 %collective-permute-start.3 = (f32[256,128]{1,0:T(8,128)S(1)}, f32[256,128]{1,0:T(8,128)S(1)}, u32[]{:S(2)}, u32[]{:S(2)}) collective-permute-start(f32[256,128]{1,0:T(8,128)S(1)} %residual.1.refs_0_), channel_id=1, source_target_pairs={{0,4},{1,5},{2,6},{3,7},{4,0},{5,1},{6,2},{7,3},{8,12},{9,13},{10,... | collective-permute-start | bytes 393224 | tf_op jit(solution)/shard_map/ppermute | solution.py:339
  45.2 2.1 %collective-permute-start.5 = (f32[256,128]{1,0:T(8,128)S(1)}, f32[256,128]{1,0:T(8,128)S(1)}, u32[]{:S(2)}, u32[]{:S(2)}) collective-permute-start(f32[256,128]{1,0:T(8,128)S(1)} %residual.1.refs_0_), channel_id=1, source_target_pairs={{0,6},{1,7},{2,4},{3,5},{4,2},{5,3},{6,0},{7,1},{8,14},{9,15},{10,... | collective-permute-start | bytes 393224 | tf_op jit(solution)/shard_map/ppermute | solution.py:339
  47.3 0.4 collective-permute-start.2
  47.6 2.3 %collective-permute-start.4 = (f32[256,128]{1,0:T(8,128)S(1)}, f32[256,128]{1,0:T(8,128)S(1)}, u32[]{:S(2)}, u32[]{:S(2)}) collective-permute-start(f32[256,128]{1,0:T(8,128)S(1)} %collective-permute-done.refs_1_), channel_id=1, source_target_pairs={{0,4},{1,5},{2,6},{3,7},{4,0},{5,1},{6,2},{7,3},{8,12},{9,13},{10,... | collective-permute-start | bytes 393224 | tf_op jit(solution)/shard_map/ppermute | solution.py:339
  49.9 2.1 %collective-permute-start.6 = (f32[256,128]{1,0:T(8,128)S(1)}, f32[256,128]{1,0:T(8,128)S(1)}, u32[]{:S(2)}, u32[]{:S(2)}) collective-permute-start(f32[256,128]{1,0:T(8,128)S(1)} %collective-permute-done.refs_1_), channel_id=1, source_target_pairs={{0,6},{1,7},{2,4},{3,5},{4,2},{5,3},{6,0},{7,1},{8,14},{9,15},{10,... | collective-permute-start | bytes 393224 | tf_op jit(solution)/shard_map/ppermute | solution.py:339
  52.0 3.9 %collective-permute-done.5.refs_6_ = f32[256,128]{1,0:T(8,128)S(1)} collective-permute-done((f32[256,128]{1,0:T(8,128)S(1)}, f32[256,128]{1,0:T(8,128)S(1)}, u32[]{:S(2)}, u32[]{:S(2)}) %collective-permute-start.5) | collective-permute-done | bytes 131104 | tf_op jit(solution)/shard_map/ppermute | solution.py:339
  56.0 1.8 collective-permute-done.6.refs_7_
  57.8 1.6 copy-done.2
  59.4 1.9 %top_solve.1 = f32[8,128,256]{2,1,0:T(8,128)S(1)} custom-call(s32[2]{0:T(128)S(1)} %pad_add_fusion.me_ref, f32[256,2048]{1,0:T(8,128)S(1)} %copy-done.2, f32[256,128]{1,0:T(8,128)S(1)} %residual.1.refs_0_, f32[256,128]{1,0:T(8,128)S(1)} %collective-permute-done.refs_1_, f32[256,128]{1,0:T(8,128)S(1)} %collective-permute-done.1.refs_2_, ...), custom_call_target="tpu_custom_call" | custom-call | tf_op jit(solution)/shard_map/top_solve/pallas_call | solution.py:123
  61.3 18.7 %all_to_all.20.parts_ref = f32[8,128,256]{2,1,0:T(8,128)S(1)} all-to-all(f32[8,128,256]{2,1,0:T(8,128)S(1)} %top_solve.1), channel_id=1, replica_groups=mesh['chip'=8,'core'=2,'y'=4,'z'=2] {'y','z'}, dimensions={0} | all-to-all | bytes 2097152 | tf_op jit(solution)/shard_map/all_to_all | solution.py:335
  80.0 1.3 collective-permute-start.7
  81.3 0.6 collective-permute-start.10
  81.9 2.7 %collective-permute-start.12 = (f32[128,256]{1,0:T(8,128)S(1)}, f32[128,256]{1,0:T(8,128)S(1)}, u32[]{:S(2)}, u32[]{:S(2)}) collective-permute-start(f32[128,256]{1,0:T(8,128)S(1)} %separator.1.own_ref), channel_id=1, source_target_pairs={{0,6},{1,7},{2,4},{3,5},{4,2},{5,3},{6,0},{7,1},{8,14},{9,15},{10,... | collective-permute-start | bytes 393224 | tf_op jit(solution)/shard_map/ppermute | solution.py:339
  84.6 0.3 collective-permute-start.8
  84.8 0.3 collective-permute-done.7.far_ref
  85.1 1.5 collective-permute-start.11
  86.6 2.7 %collective-permute-start.13 = (f32[128,256]{1,0:T(8,128)S(1)}, f32[128,256]{1,0:T(8,128)S(1)}, u32[]{:S(2)}, u32[]{:S(2)}) collective-permute-start(f32[128,256]{1,0:T(8,128)S(1)} %collective-permute-done.7.far_ref), channel_id=1, source_target_pairs={{0,6},{1,7},{2,4},{3,5},{4,2},{5,3},{6,0},{7,1},{8,14},{9,15},{10,... | collective-permute-start | bytes 393224 | tf_op jit(solution)/shard_map/ppermute | solution.py:339
  89.3 1.0 fusion.1
  90.4 6.4 %leaf_near.1.refs_6_ = f32[8,128,256]{2,1,0:T(8,128)S(1)} custom-call(s32[2]{0:T(128)S(1)} %pad_add_fusion.me_ref, f32[128,256]{1,0:T(8,128)S(1)} %separator.1.own_ref, f32[128,256]{1,0:T(8,128)S(1)} %collective-permute-done.7.far_ref, f32[8,128,256]{2,1,0:T(8,128)S(1)} %copy-done.4, f32[8,2048,256]{2,1,0:T(8,128)} %refs_9_.1), custom_call_target="tpu_custom_call" | custom-call | flops 1000000000 | bytes 6000000 | tf_op jit(solution)/shard_map/leaf_near/pallas_call | solution.py:166
  96.9 10.4 %leaf_back.1 = f32[2048,128]{1,0:T(8,128)S(1)} custom-call(s32[2]{0:T(128)S(1)} %pad_add_fusion.me_ref, f32[128,256]{1,0:T(8,128)S(1)} %collective-permute-done.8.refs_0_, f32[128,256]{1,0:T(8,128)S(1)} %collective-permute-done.9.refs_1_, f32[128,256]{1,0:T(8,128)S(1)} %collective-permute-done.10.refs_2_, f32[128,256]{1,0:T(8,128)S(1)} %collective-permute-done.11.refs_3_, ...), custom_call_target="tpu_custom_call" | custom-call | tf_op jit(solution)/shard_map/leaf_back/pallas_call | solution.py:211
  107.3 24.1 %all_to_all.21 = f32[64,32,128]{2,1,0:T(8,128)S(1)} all-to-all(f32[64,32,128]{2,1,0:T(8,128)S(1)} %bitcast.16), channel_id=1, replica_groups=mesh['chip'=8,'core'=2,'y'=4,'z'=2] {'chip','y','z'}, dimensions={0} | all-to-all | bytes 2097152 | tf_op jit(solution)/shard_map/all_to_all | solution.py:371
  131.4 2.7 %collective-permute-done.14.other_ref = f32[8,256,128]{2,1,0:T(8,128)S(1)} collective-permute-done((f32[8,256,128]{2,1,0:T(8,128)S(1)}, f32[8,256,128]{2,1,0:T(8,128)S(1)}, u32[]{:S(2)}, u32[]{:S(2)}) %collective-permute-start.14) | collective-permute-done | bytes 1048608 | tf_op jit(solution)/shard_map/ppermute | solution.py:373
  134.0 16.7 %select_quads.1 = f32[64,32,128]{2,1,0:T(8,128)S(1)} custom-call(s32[1]{0:T(128)} %bitcast.core_ref, s32[16384]{0:T(1024)S(1)} %bitcast.19, f32[512,512]{1,0:T(8,128)S(1)} %copy-done.3, f32[8,256,128]{2,1,0:T(8,128)S(1)} %bitcast.15, f32[8,256,128]{2,1,0:T(8,128)S(1)} %collective-permute-done.14.other_ref), custom_call_target="tpu_custom_call" | custom-call | tf_op jit(solution)/shard_map/select_quads/pallas_call | solution.py:287
  150.8 23.5 %all_to_all.22 = f32[64,32,128]{2,1,0:T(8,128)S(1)} all-to-all(f32[64,32,128]{2,1,0:T(8,128)S(1)} %select_quads.1), channel_id=1, replica_groups=mesh['chip'=8,'core'=2,'y'=4,'z'=2] {'chip','y','z'}, dimensions={0} | all-to-all | bytes 2097152 | tf_op jit(solution)/shard_map/all_to_all | solution.py:375
  174.3 1.9 %assemble_sens.1 = f32[2,4,64,512]{3,2,1,0:T(8,128)} custom-call(f32[2048,128]{1,0:T(8,128)S(1)} %bitcast.17), custom_call_target="tpu_custom_call" | custom-call | tf_op jit(solution)/shard_map/assemble_sens/pallas_call | solution.py:323
  (38 shorter events, 0.4 us)
Async XLA Ops:
  6.5 20.2 %copy-start = (f32[2048,128]{1,0:T(8,128)S(1)}, f32[2048,128]{1,0:T(8,128)}, u32[]{:S(2)}) copy-start(f32[2048,128]{1,0:T(8,128)} %param.9) | copy-start | bytes 3145732
  19.8 6.1 %copy-start.7 = (s32[512,4]{0,1:T(4,128)S(1)}, s32[512,4]{0,1:T(4,128)}, u32[]{:S(2)}) copy-start(s32[512,4]{0,1:T(4,128)} %param.14) | copy-start | bytes 24580
  19.8 6.2 %copy-start.6 = (s32[16,512]{1,0:T(8,128)S(1)}, s32[16,512]{1,0:T(8,128)}, u32[]{:S(2)}) copy-start(s32[16,512]{1,0:T(8,128)} %param.15) | copy-start | bytes 98308
  19.8 21.9 %all-to-all-start = ((f32[8,256,128]{2,1,0:T(8,128)}), f32[8,256,128]{2,1,0:T(8,128)S(1)}, u32[]{:S(2)}, u32[]{:S(2)}) async-start(f32[8,256,128]{2,1,0:T(8,128)} %bitcast.20), calls=%async_computation | async-start | bytes 2097152 | tf_op jit(solution)/shard_map/all_to_all | solution.py:335
  25.8 63.5 %all-gather.2.cloned.1.call-start = ((), (), s32[]{:S(2)}) async-start(), calls=%async_computation.4 | async-start | bytes 1114112 | tf_op jit(solution)/shard_map/all_gather | solution.py:359
  41.7 5.5 %collective-permute-start = (f32[256,128]{1,0:T(8,128)S(1)}, f32[256,128]{1,0:T(8,128)S(1)}, u32[]{:S(2)}, u32[]{:S(2)}) collective-permute-start(f32[256,128]{1,0:T(8,128)S(1)} %residual.1.refs_0_), channel_id=1, source_target_pairs={{0,1},{1,0},{2,3},{3,2},{4,5},{5,4},{6,7},{7,6},{8,9},{9,8},{10,11... | collective-permute-start | bytes 393224 | tf_op jit(solution)/shard_map/ppermute | solution.py:343
  42.6 7.3 %collective-permute-start.1 = (f32[256,128]{1,0:T(8,128)S(1)}, f32[256,128]{1,0:T(8,128)S(1)}, u32[]{:S(2)}, u32[]{:S(2)}) collective-permute-start(f32[256,128]{1,0:T(8,128)S(1)} %residual.1.refs_0_), channel_id=1, source_target_pairs={{0,2},{1,3},{2,0},{3,1},{4,6},{5,7},{6,4},{7,5},{8,10},{9,11},{10,... | collective-permute-start | bytes 393224 | tf_op jit(solution)/shard_map/ppermute | solution.py:339
  43.1 8.9 %collective-permute-start.3 = (f32[256,128]{1,0:T(8,128)S(1)}, f32[256,128]{1,0:T(8,128)S(1)}, u32[]{:S(2)}, u32[]{:S(2)}) collective-permute-start(f32[256,128]{1,0:T(8,128)S(1)} %residual.1.refs_0_), channel_id=1, source_target_pairs={{0,4},{1,5},{2,6},{3,7},{4,0},{5,1},{6,2},{7,3},{8,12},{9,13},{10,... | collective-permute-start | bytes 393224 | tf_op jit(solution)/shard_map/ppermute | solution.py:339
  45.2 10.8 %collective-permute-start.5 = (f32[256,128]{1,0:T(8,128)S(1)}, f32[256,128]{1,0:T(8,128)S(1)}, u32[]{:S(2)}, u32[]{:S(2)}) collective-permute-start(f32[256,128]{1,0:T(8,128)S(1)} %residual.1.refs_0_), channel_id=1, source_target_pairs={{0,6},{1,7},{2,4},{3,5},{4,2},{5,3},{6,0},{7,1},{8,14},{9,15},{10,... | collective-permute-start | bytes 393224 | tf_op jit(solution)/shard_map/ppermute | solution.py:339
  47.3 8.7 %collective-permute-start.2 = (f32[256,128]{1,0:T(8,128)S(1)}, f32[256,128]{1,0:T(8,128)S(1)}, u32[]{:S(2)}, u32[]{:S(2)}) collective-permute-start(f32[256,128]{1,0:T(8,128)S(1)} %collective-permute-done.refs_1_), channel_id=1, source_target_pairs={{0,2},{1,3},{2,0},{3,1},{4,6},{5,7},{6,4},{7,5},{8,10},{9,11},{10,... | collective-permute-start | bytes 393224 | tf_op jit(solution)/shard_map/ppermute | solution.py:339
  47.6 8.4 %collective-permute-start.4 = (f32[256,128]{1,0:T(8,128)S(1)}, f32[256,128]{1,0:T(8,128)S(1)}, u32[]{:S(2)}, u32[]{:S(2)}) collective-permute-start(f32[256,128]{1,0:T(8,128)S(1)} %collective-permute-done.refs_1_), channel_id=1, source_target_pairs={{0,4},{1,5},{2,6},{3,7},{4,0},{5,1},{6,2},{7,3},{8,12},{9,13},{10,... | collective-permute-start | bytes 393224 | tf_op jit(solution)/shard_map/ppermute | solution.py:339
  49.9 7.9 %collective-permute-start.6 = (f32[256,128]{1,0:T(8,128)S(1)}, f32[256,128]{1,0:T(8,128)S(1)}, u32[]{:S(2)}, u32[]{:S(2)}) collective-permute-start(f32[256,128]{1,0:T(8,128)S(1)} %collective-permute-done.refs_1_), channel_id=1, source_target_pairs={{0,6},{1,7},{2,4},{3,5},{4,2},{5,3},{6,0},{7,1},{8,14},{9,15},{10,... | collective-permute-start | bytes 393224 | tf_op jit(solution)/shard_map/ppermute | solution.py:339
  57.8 1.6 copy-start.2
  61.3 29.1 %copy-start.4 = (f32[8,128,256]{2,1,0:T(8,128)S(1)}, f32[8,128,256]{2,1,0:T(8,128)}, u32[]{:S(2)}) copy-start(f32[8,128,256]{2,1,0:T(8,128)} %get-tuple-element.30.forward_ref) | copy-start | bytes 3145732
  80.0 5.0 %collective-permute-start.7 = (f32[128,256]{1,0:T(8,128)S(1)}, f32[128,256]{1,0:T(8,128)S(1)}, u32[]{:S(2)}, u32[]{:S(2)}) collective-permute-start(f32[128,256]{1,0:T(8,128)S(1)} %separator.1.own_ref), channel_id=1, source_target_pairs={{0,1},{1,0},{2,3},{3,2},{4,5},{5,4},{6,7},{7,6},{8,9},{9,8},{10,11... | collective-permute-start | bytes 393224 | tf_op jit(solution)/shard_map/ppermute | solution.py:343
  81.3 8.0 %collective-permute-start.10 = (f32[128,256]{1,0:T(8,128)S(1)}, f32[128,256]{1,0:T(8,128)S(1)}, u32[]{:S(2)}, u32[]{:S(2)}) collective-permute-start(f32[128,256]{1,0:T(8,128)S(1)} %separator.1.own_ref), channel_id=1, source_target_pairs={{0,4},{1,5},{2,6},{3,7},{4,0},{5,1},{6,2},{7,3},{8,12},{9,13},{10,... | collective-permute-start | bytes 393224 | tf_op jit(solution)/shard_map/ppermute | solution.py:339
  81.9 15.0 %collective-permute-start.12 = (f32[128,256]{1,0:T(8,128)S(1)}, f32[128,256]{1,0:T(8,128)S(1)}, u32[]{:S(2)}, u32[]{:S(2)}) collective-permute-start(f32[128,256]{1,0:T(8,128)S(1)} %separator.1.own_ref), channel_id=1, source_target_pairs={{0,6},{1,7},{2,4},{3,5},{4,2},{5,3},{6,0},{7,1},{8,14},{9,15},{10,... | collective-permute-start | bytes 393224 | tf_op jit(solution)/shard_map/ppermute | solution.py:339
  84.6 12.3 %collective-permute-start.8 = (f32[128,256]{1,0:T(8,128)S(1)}, f32[128,256]{1,0:T(8,128)S(1)}, u32[]{:S(2)}, u32[]{:S(2)}) collective-permute-start(f32[128,256]{1,0:T(8,128)S(1)} %separator.1.own_ref), channel_id=1, source_target_pairs={{0,2},{1,3},{2,0},{3,1},{4,6},{5,7},{6,4},{7,5},{8,10},{9,11},{10,... | collective-permute-start | bytes 393224 | tf_op jit(solution)/shard_map/ppermute | solution.py:339
  85.1 11.8 %collective-permute-start.11 = (f32[128,256]{1,0:T(8,128)S(1)}, f32[128,256]{1,0:T(8,128)S(1)}, u32[]{:S(2)}, u32[]{:S(2)}) collective-permute-start(f32[128,256]{1,0:T(8,128)S(1)} %collective-permute-done.7.far_ref), channel_id=1, source_target_pairs={{0,4},{1,5},{2,6},{3,7},{4,0},{5,1},{6,2},{7,3},{8,12},{9,13},{10,... | collective-permute-start | bytes 393224 | tf_op jit(solution)/shard_map/ppermute | solution.py:339
  86.6 10.3 %collective-permute-start.13 = (f32[128,256]{1,0:T(8,128)S(1)}, f32[128,256]{1,0:T(8,128)S(1)}, u32[]{:S(2)}, u32[]{:S(2)}) collective-permute-start(f32[128,256]{1,0:T(8,128)S(1)} %collective-permute-done.7.far_ref), channel_id=1, source_target_pairs={{0,6},{1,7},{2,4},{3,5},{4,2},{5,3},{6,0},{7,1},{8,14},{9,15},{10,... | collective-permute-start | bytes 393224 | tf_op jit(solution)/shard_map/ppermute | solution.py:339
  89.3 7.6 %collective-permute-start.9 = (f32[128,256]{1,0:T(8,128)S(1)}, f32[128,256]{1,0:T(8,128)S(1)}, u32[]{:S(2)}, u32[]{:S(2)}) collective-permute-start(f32[128,256]{1,0:T(8,128)S(1)} %collective-permute-done.7.far_ref), channel_id=1, source_target_pairs={{0,2},{1,3},{2,0},{3,1},{4,6},{5,7},{6,4},{7,5},{8,10},{9,11},{10,... | collective-permute-start | bytes 393224 | tf_op jit(solution)/shard_map/ppermute | solution.py:339
  90.4 6.5 %copy-start.1 = (f32[8,256,256]{2,1,0:T(8,128)S(1)}, f32[8,256,256]{2,1,0:T(8,128)}, u32[]{:S(2)}) copy-start(f32[8,256,256]{2,1,0:T(8,128)} %refs_10_.1) | copy-start | bytes 6291460
  90.4 6.5 %copy-start.5 = (f32[8,256]{1,0:T(8,128)S(1)}, f32[8,256]{1,0:T(8,128)}, u32[]{:S(2)}) copy-start(f32[8,256]{1,0:T(8,128)} %refs_11_.1) | copy-start | bytes 24580
  107.3 26.7 %copy-start.3 = (f32[512,512]{1,0:T(8,128)S(1)}, f32[512,512]{1,0:T(8,128)}, u32[]{:S(2)}) copy-start(f32[512,512]{1,0:T(8,128)} %all-gather.2.cloned.1.call-done.lists_ref) | copy-start | bytes 3145732
  131.4 2.7 %collective-permute-start.14 = (f32[8,256,128]{2,1,0:T(8,128)S(1)}, f32[8,256,128]{2,1,0:T(8,128)S(1)}, u32[]{:S(2)}, u32[]{:S(2)}) collective-permute-start(f32[8,256,128]{2,1,0:T(8,128)S(1)} %bitcast.14), channel_id=1, source_target_pairs={{0,8},{8,0},{1,9},{9,1},{2,10},{10,2},{3,11},{11,3},{4,12},{12,4},... | collective-permute-start | bytes 3145736 | tf_op jit(solution)/shard_map/ppermute | solution.py:373
Sparse Core Ops, SparseCore 0:
  29.1 47.3 all-gather.1

commit v6 on v5

--- a/solution.py
+++ b/solution.py
@@ -155,7 +155,8 @@
     def _():
         store_split(me_ref, (own_ref, far_ref), split_ref)
 
-    out_ref[0] = minus_terms(forward_ref[0], split_ref, (coupling_ref,))
+    for b in range(2):
+        out_ref[b] = minus_terms(forward_ref[b], split_ref, (coupling_ref.at[b : b + 1],))
 
 
 def panels(dy):
@@ -167,10 +168,11 @@
         near_kernel,
         grid_spec=pltpu.PrefetchScalarGridSpec(
             num_scalar_prefetch=1,
-            grid=(8,),
+            grid=(4,),
             in_specs=[pl.BlockSpec((128, 256), lambda j, me: (0, 0))] * 2
-            + [pl.BlockSpec((1, 128, 256), lambda j, me: (j, 0, 0)), panels(0)],
-            out_specs=pl.BlockSpec((1, 128, 256), lambda j, me: (j, 0, 0)),
+            + [pl.BlockSpec((2, 128, 256), lambda j, me: (j, 0, 0))]
+            + [pl.BlockSpec((2, 512, 256), lambda j, me: (j, me[0], 0))],
+            out_specs=pl.BlockSpec((2, 128, 256), lambda j, me: (j, 0, 0)),
             scratch_shapes=[pltpu.VMEM((256, 512), jnp.bfloat16)],
         ),
         out_shape=jax.ShapeDtypeStruct((8, 128, 256), jnp.float32),

time: 184 us -> 183 us (level)
  Pallas kernels: 50.7 us -> 48.6 us
    pallas_call x1, Pallas kernels: 6.44 us -> 4.37 us  [near(): pl.pallas_call(near_kernel, grid_spec=pltpu.PrefetchScalarGridSpec(num_sc...]
  transfers between devices with their start and end apart: 17 -> 17, of which waited for: 5 -> 5; matrix products, arithmetic and copies ran while one was open for 1% -> 1% of each run, Pallas kernels for 5% -> 3%
where the time goes in v6:
time: 183 us; the launch traced here: 182 us
  blocking collectives  67.4 us (37%)
  Pallas kernels  48.6 us (27%)
  starting transfers between devices  25.3 us (14%)
  waiting for transfers between devices  23.7 us (13%)
  between operations  13.6 us (7%)
    all_to_all x1, blocking collectives, local(): lax.all_to_all(fields.reshape(CHIPS, 32, 128), ('chip', 'y', 'z'), 0, 0,...  25.2 us
    all_to_all x1, blocking collectives, local(): received = lax.all_to_all(picked, ('chip', 'y', 'z'), 0, 0, tiled=True)  23.6 us
    all_to_all x1, blocking collectives, exchange(): return lax.all_to_all(parts, ('y', 'z'), 0, 0, tiled=True)  18.7 us
    ppermute x12, starting transfers between devices, send(): return lax.ppermute(value, ('y', 'z'), [(i, i ^ d) for i in range(8)])  17.1 us
    pallas_call x1, Pallas kernels, select(): pl.pallas_call(select_kernel, grid_spec=pltpu.PrefetchScalarGridSpec(num_...  16.8 us
    all_to_all x1, waiting for transfers between devices, exchange(): return lax.all_to_all(parts, ('y', 'z'), 0, 0, tiled=True)  14.9 us
    pallas_call x1, Pallas kernels, front(): pl.pallas_call(front_kernel, grid=(8,), out_shape=(jax.ShapeDtypeStruct((...  13.2 us
    pallas_call x1, Pallas kernels, back(): pl.pallas_call(back_kernel, grid_spec=pltpu.PrefetchScalarGridSpec(num_sc...  10.4 us
  transfers between devices with their start and end apart: 17, of which 5 were waited for; matrix products, arithmetic and copies ran while one was open for 1% of the time, Pallas kernels for 3%

profile of v6, /device:TPU:0, one launch (start us, length us, event | category | flops | bytes accessed | tf_op | source)
XLA Modules:
  0.0 182.1 jit_solution(4791614437056983721)
XLA Ops:
  6.5 13.2 %leaf_front.1 = (f32[2048,128]{1,0:T(8,128)}, f32[8,128,256]{2,1,0:T(8,128)}) custom-call(f32[8,256,256]{2,1,0:T(8,128)} %refs_10_.1, f32[8,256,128]{2,1,0:T(8,128)} %rhs_ref.1, f32[8,2048,256]{2,1,0:T(8,128)} %refs_9_.1), custom_call_target="tpu_custom_call" | custom-call | tf_op jit(solution)/shard_map/leaf_front/pallas_call | solution.py:51
  19.8 6.1 %all-to-all-start = ((f32[8,256,128]{2,1,0:T(8,128)}), f32[8,256,128]{2,1,0:T(8,128)S(1)}, u32[]{:S(2)}, u32[]{:S(2)}) async-start(f32[8,256,128]{2,1,0:T(8,128)} %bitcast.20), calls=%async_computation | async-start | bytes 2097152 | tf_op jit(solution)/shard_map/all_to_all | solution.py:337
  25.9 0.1 pad.2.clone
  26.0 0.7 add_convert_fusion
  26.7 14.9 %all-to-all-done.parts_ref = f32[8,256,128]{2,1,0:T(8,128)S(1)} async-done(((f32[8,256,128]{2,1,0:T(8,128)}), f32[8,256,128]{2,1,0:T(8,128)S(1)}, u32[]{:S(2)}, u32[]{:S(2)}) %all-to-all-start) | async-done | bytes 1048608 | tf_op jit(solution)/shard_map/all_to_all | solution.py:337
  41.7 0.8 collective-permute-start
  42.6 0.6 collective-permute-start.1
  43.1 2.1 %collective-permute-start.3 = (f32[256,128]{1,0:T(8,128)S(1)}, f32[256,128]{1,0:T(8,128)S(1)}, u32[]{:S(2)}, u32[]{:S(2)}) collective-permute-start(f32[256,128]{1,0:T(8,128)S(1)} %residual.1.refs_0_), channel_id=1, source_target_pairs={{0,4},{1,5},{2,6},{3,7},{4,0},{5,1},{6,2},{7,3},{8,12},{9,13},{10,... | collective-permute-start | bytes 393224 | tf_op jit(solution)/shard_map/ppermute | solution.py:341
  45.2 2.1 %collective-permute-start.5 = (f32[256,128]{1,0:T(8,128)S(1)}, f32[256,128]{1,0:T(8,128)S(1)}, u32[]{:S(2)}, u32[]{:S(2)}) collective-permute-start(f32[256,128]{1,0:T(8,128)S(1)} %residual.1.refs_0_), channel_id=1, source_target_pairs={{0,6},{1,7},{2,4},{3,5},{4,2},{5,3},{6,0},{7,1},{8,14},{9,15},{10,... | collective-permute-start | bytes 393224 | tf_op jit(solution)/shard_map/ppermute | solution.py:341
  47.3 0.4 collective-permute-start.2
  47.6 2.3 %collective-permute-start.4 = (f32[256,128]{1,0:T(8,128)S(1)}, f32[256,128]{1,0:T(8,128)S(1)}, u32[]{:S(2)}, u32[]{:S(2)}) collective-permute-start(f32[256,128]{1,0:T(8,128)S(1)} %collective-permute-done.refs_1_), channel_id=1, source_target_pairs={{0,4},{1,5},{2,6},{3,7},{4,0},{5,1},{6,2},{7,3},{8,12},{9,13},{10,... | collective-permute-start | bytes 393224 | tf_op jit(solution)/shard_map/ppermute | solution.py:341
  49.9 2.1 %collective-permute-start.6 = (f32[256,128]{1,0:T(8,128)S(1)}, f32[256,128]{1,0:T(8,128)S(1)}, u32[]{:S(2)}, u32[]{:S(2)}) collective-permute-start(f32[256,128]{1,0:T(8,128)S(1)} %collective-permute-done.refs_1_), channel_id=1, source_target_pairs={{0,6},{1,7},{2,4},{3,5},{4,2},{5,3},{6,0},{7,1},{8,14},{9,15},{10,... | collective-permute-start | bytes 393224 | tf_op jit(solution)/shard_map/ppermute | solution.py:341
  52.0 3.9 %collective-permute-done.5.refs_6_ = f32[256,128]{1,0:T(8,128)S(1)} collective-permute-done((f32[256,128]{1,0:T(8,128)S(1)}, f32[256,128]{1,0:T(8,128)S(1)}, u32[]{:S(2)}, u32[]{:S(2)}) %collective-permute-start.5) | collective-permute-done | bytes 131104 | tf_op jit(solution)/shard_map/ppermute | solution.py:341
  56.0 1.8 collective-permute-done.6.refs_7_
  57.8 1.6 copy-done.2
  59.4 1.9 %top_solve.1 = f32[8,128,256]{2,1,0:T(8,128)S(1)} custom-call(s32[2]{0:T(128)S(1)} %pad_add_fusion.me_ref, f32[256,2048]{1,0:T(8,128)S(1)} %copy-done.2, f32[256,128]{1,0:T(8,128)S(1)} %residual.1.refs_0_, f32[256,128]{1,0:T(8,128)S(1)} %collective-permute-done.refs_1_, f32[256,128]{1,0:T(8,128)S(1)} %collective-permute-done.1.refs_2_, ...), custom_call_target="tpu_custom_call" | custom-call | tf_op jit(solution)/shard_map/top_solve/pallas_call | solution.py:123
  61.3 18.7 %all_to_all.20.parts_ref = f32[8,128,256]{2,1,0:T(8,128)S(1)} all-to-all(f32[8,128,256]{2,1,0:T(8,128)S(1)} %top_solve.1), channel_id=1, replica_groups=mesh['chip'=8,'core'=2,'y'=4,'z'=2] {'y','z'}, dimensions={0} | all-to-all | bytes 2097152 | tf_op jit(solution)/shard_map/all_to_all | solution.py:337
  80.0 1.3 collective-permute-start.7
  81.3 0.6 collective-permute-start.10
  81.9 2.7 %collective-permute-start.12 = (f32[128,256]{1,0:T(8,128)S(1)}, f32[128,256]{1,0:T(8,128)S(1)}, u32[]{:S(2)}, u32[]{:S(2)}) collective-permute-start(f32[128,256]{1,0:T(8,128)S(1)} %separator.1.own_ref), channel_id=1, source_target_pairs={{0,6},{1,7},{2,4},{3,5},{4,2},{5,3},{6,0},{7,1},{8,14},{9,15},{10,... | collective-permute-start | bytes 393224 | tf_op jit(solution)/shard_map/ppermute | solution.py:341
  84.6 0.3 collective-permute-start.8
  84.8 0.3 collective-permute-done.7.far_ref
  85.1 1.5 collective-permute-start.11
  86.6 2.7 %collective-permute-start.13 = (f32[128,256]{1,0:T(8,128)S(1)}, f32[128,256]{1,0:T(8,128)S(1)}, u32[]{:S(2)}, u32[]{:S(2)}) collective-permute-start(f32[128,256]{1,0:T(8,128)S(1)} %collective-permute-done.7.far_ref), channel_id=1, source_target_pairs={{0,6},{1,7},{2,4},{3,5},{4,2},{5,3},{6,0},{7,1},{8,14},{9,15},{10,... | collective-permute-start | bytes 393224 | tf_op jit(solution)/shard_map/ppermute | solution.py:341
  89.3 1.0 fusion.1
  90.4 4.4 %leaf_near.1.refs_6_ = f32[8,128,256]{2,1,0:T(8,128)S(1)} custom-call(s32[2]{0:T(128)S(1)} %pad_add_fusion.me_ref, f32[128,256]{1,0:T(8,128)S(1)} %separator.1.own_ref, f32[128,256]{1,0:T(8,128)S(1)} %collective-permute-done.7.far_ref, f32[8,128,256]{2,1,0:T(8,128)S(1)} %copy-done.4, f32[8,2048,256]{2,1,0:T(8,128)} %refs_9_.1), custom_call_target="tpu_custom_call" | custom-call | flops 1000000000 | bytes 6000000 | tf_op jit(solution)/shard_map/leaf_near/pallas_call | solution.py:167
  94.9 10.4 %leaf_back.1 = f32[2048,128]{1,0:T(8,128)S(1)} custom-call(s32[2]{0:T(128)S(1)} %pad_add_fusion.me_ref, f32[128,256]{1,0:T(8,128)S(1)} %collective-permute-done.8.refs_0_, f32[128,256]{1,0:T(8,128)S(1)} %collective-permute-done.9.refs_1_, f32[128,256]{1,0:T(8,128)S(1)} %collective-permute-done.10.refs_2_, f32[128,256]{1,0:T(8,128)S(1)} %collective-permute-done.11.refs_3_, ...), custom_call_target="tpu_custom_call" | custom-call | tf_op jit(solution)/shard_map/leaf_back/pallas_call | solution.py:213
  105.2 25.2 %all_to_all.21 = f32[64,32,128]{2,1,0:T(8,128)S(1)} all-to-all(f32[64,32,128]{2,1,0:T(8,128)S(1)} %bitcast.16), channel_id=1, replica_groups=mesh['chip'=8,'core'=2,'y'=4,'z'=2] {'chip','y','z'}, dimensions={0} | all-to-all | bytes 2097152 | tf_op jit(solution)/shard_map/all_to_all | solution.py:373
  130.4 2.7 %collective-permute-done.14.other_ref = f32[8,256,128]{2,1,0:T(8,128)S(1)} collective-permute-done((f32[8,256,128]{2,1,0:T(8,128)S(1)}, f32[8,256,128]{2,1,0:T(8,128)S(1)}, u32[]{:S(2)}, u32[]{:S(2)}) %collective-permute-start.14) | collective-permute-done | bytes 1048608 | tf_op jit(solution)/shard_map/ppermute | solution.py:375
  133.0 16.8 %select_quads.1 = f32[64,32,128]{2,1,0:T(8,128)S(1)} custom-call(s32[1]{0:T(128)} %bitcast.core_ref, s32[16384]{0:T(1024)S(1)} %bitcast.19, f32[512,512]{1,0:T(8,128)S(1)} %copy-done.3, f32[8,256,128]{2,1,0:T(8,128)S(1)} %bitcast.15, f32[8,256,128]{2,1,0:T(8,128)S(1)} %collective-permute-done.14.other_ref), custom_call_target="tpu_custom_call" | custom-call | tf_op jit(solution)/shard_map/select_quads/pallas_call | solution.py:289
  149.8 23.6 %all_to_all.22 = f32[64,32,128]{2,1,0:T(8,128)S(1)} all-to-all(f32[64,32,128]{2,1,0:T(8,128)S(1)} %select_quads.1), channel_id=1, replica_groups=mesh['chip'=8,'core'=2,'y'=4,'z'=2] {'chip','y','z'}, dimensions={0} | all-to-all | bytes 2097152 | tf_op jit(solution)/shard_map/all_to_all | solution.py:377
  173.4 1.9 %assemble_sens.1 = f32[2,4,64,512]{3,2,1,0:T(8,128)} custom-call(f32[2048,128]{1,0:T(8,128)S(1)} %bitcast.17), custom_call_target="tpu_custom_call" | custom-call | tf_op jit(solution)/shard_map/assemble_sens/pallas_call | solution.py:325
  (38 shorter events, 0.4 us)
Async XLA Ops:
  6.5 20.2 %copy-start = (f32[2048,128]{1,0:T(8,128)S(1)}, f32[2048,128]{1,0:T(8,128)}, u32[]{:S(2)}) copy-start(f32[2048,128]{1,0:T(8,128)} %param.9) | copy-start | bytes 3145732
  19.8 6.1 %copy-start.7 = (s32[512,4]{0,1:T(4,128)S(1)}, s32[512,4]{0,1:T(4,128)}, u32[]{:S(2)}) copy-start(s32[512,4]{0,1:T(4,128)} %param.14) | copy-start | bytes 24580
  19.8 6.2 %copy-start.6 = (s32[16,512]{1,0:T(8,128)S(1)}, s32[16,512]{1,0:T(8,128)}, u32[]{:S(2)}) copy-start(s32[16,512]{1,0:T(8,128)} %param.15) | copy-start | bytes 98308
  19.8 21.9 %all-to-all-start = ((f32[8,256,128]{2,1,0:T(8,128)}), f32[8,256,128]{2,1,0:T(8,128)S(1)}, u32[]{:S(2)}, u32[]{:S(2)}) async-start(f32[8,256,128]{2,1,0:T(8,128)} %bitcast.20), calls=%async_computation | async-start | bytes 2097152 | tf_op jit(solution)/shard_map/all_to_all | solution.py:337
  25.8 63.5 %all-gather.2.cloned.1.call-start = ((), (), s32[]{:S(2)}) async-start(), calls=%async_computation.4 | async-start | bytes 1114112 | tf_op jit(solution)/shard_map/all_gather | solution.py:361
  41.7 5.5 %collective-permute-start = (f32[256,128]{1,0:T(8,128)S(1)}, f32[256,128]{1,0:T(8,128)S(1)}, u32[]{:S(2)}, u32[]{:S(2)}) collective-permute-start(f32[256,128]{1,0:T(8,128)S(1)} %residual.1.refs_0_), channel_id=1, source_target_pairs={{0,1},{1,0},{2,3},{3,2},{4,5},{5,4},{6,7},{7,6},{8,9},{9,8},{10,11... | collective-permute-start | bytes 393224 | tf_op jit(solution)/shard_map/ppermute | solution.py:345
  42.6 7.3 %collective-permute-start.1 = (f32[256,128]{1,0:T(8,128)S(1)}, f32[256,128]{1,0:T(8,128)S(1)}, u32[]{:S(2)}, u32[]{:S(2)}) collective-permute-start(f32[256,128]{1,0:T(8,128)S(1)} %residual.1.refs_0_), channel_id=1, source_target_pairs={{0,2},{1,3},{2,0},{3,1},{4,6},{5,7},{6,4},{7,5},{8,10},{9,11},{10,... | collective-permute-start | bytes 393224 | tf_op jit(solution)/shard_map/ppermute | solution.py:341
  43.1 8.9 %collective-permute-start.3 = (f32[256,128]{1,0:T(8,128)S(1)}, f32[256,128]{1,0:T(8,128)S(1)}, u32[]{:S(2)}, u32[]{:S(2)}) collective-permute-start(f32[256,128]{1,0:T(8,128)S(1)} %residual.1.refs_0_), channel_id=1, source_target_pairs={{0,4},{1,5},{2,6},{3,7},{4,0},{5,1},{6,2},{7,3},{8,12},{9,13},{10,... | collective-permute-start | bytes 393224 | tf_op jit(solution)/shard_map/ppermute | solution.py:341
  45.2 10.8 %collective-permute-start.5 = (f32[256,128]{1,0:T(8,128)S(1)}, f32[256,128]{1,0:T(8,128)S(1)}, u32[]{:S(2)}, u32[]{:S(2)}) collective-permute-start(f32[256,128]{1,0:T(8,128)S(1)} %residual.1.refs_0_), channel_id=1, source_target_pairs={{0,6},{1,7},{2,4},{3,5},{4,2},{5,3},{6,0},{7,1},{8,14},{9,15},{10,... | collective-permute-start | bytes 393224 | tf_op jit(solution)/shard_map/ppermute | solution.py:341
  47.3 8.7 %collective-permute-start.2 = (f32[256,128]{1,0:T(8,128)S(1)}, f32[256,128]{1,0:T(8,128)S(1)}, u32[]{:S(2)}, u32[]{:S(2)}) collective-permute-start(f32[256,128]{1,0:T(8,128)S(1)} %collective-permute-done.refs_1_), channel_id=1, source_target_pairs={{0,2},{1,3},{2,0},{3,1},{4,6},{5,7},{6,4},{7,5},{8,10},{9,11},{10,... | collective-permute-start | bytes 393224 | tf_op jit(solution)/shard_map/ppermute | solution.py:341
  47.6 8.4 %collective-permute-start.4 = (f32[256,128]{1,0:T(8,128)S(1)}, f32[256,128]{1,0:T(8,128)S(1)}, u32[]{:S(2)}, u32[]{:S(2)}) collective-permute-start(f32[256,128]{1,0:T(8,128)S(1)} %collective-permute-done.refs_1_), channel_id=1, source_target_pairs={{0,4},{1,5},{2,6},{3,7},{4,0},{5,1},{6,2},{7,3},{8,12},{9,13},{10,... | collective-permute-start | bytes 393224 | tf_op jit(solution)/shard_map/ppermute | solution.py:341
  49.9 7.9 %collective-permute-start.6 = (f32[256,128]{1,0:T(8,128)S(1)}, f32[256,128]{1,0:T(8,128)S(1)}, u32[]{:S(2)}, u32[]{:S(2)}) collective-permute-start(f32[256,128]{1,0:T(8,128)S(1)} %collective-permute-done.refs_1_), channel_id=1, source_target_pairs={{0,6},{1,7},{2,4},{3,5},{4,2},{5,3},{6,0},{7,1},{8,14},{9,15},{10,... | collective-permute-start | bytes 393224 | tf_op jit(solution)/shard_map/ppermute | solution.py:341
  57.8 1.6 copy-start.2
  61.3 29.1 %copy-start.4 = (f32[8,128,256]{2,1,0:T(8,128)S(1)}, f32[8,128,256]{2,1,0:T(8,128)}, u32[]{:S(2)}) copy-start(f32[8,128,256]{2,1,0:T(8,128)} %get-tuple-element.30.forward_ref) | copy-start | bytes 3145732
  80.0 5.0 %collective-permute-start.7 = (f32[128,256]{1,0:T(8,128)S(1)}, f32[128,256]{1,0:T(8,128)S(1)}, u32[]{:S(2)}, u32[]{:S(2)}) collective-permute-start(f32[128,256]{1,0:T(8,128)S(1)} %separator.1.own_ref), channel_id=1, source_target_pairs={{0,1},{1,0},{2,3},{3,2},{4,5},{5,4},{6,7},{7,6},{8,9},{9,8},{10,11... | collective-permute-start | bytes 393224 | tf_op jit(solution)/shard_map/ppermute | solution.py:345
  81.3 8.0 %collective-permute-start.10 = (f32[128,256]{1,0:T(8,128)S(1)}, f32[128,256]{1,0:T(8,128)S(1)}, u32[]{:S(2)}, u32[]{:S(2)}) collective-permute-start(f32[128,256]{1,0:T(8,128)S(1)} %separator.1.own_ref), channel_id=1, source_target_pairs={{0,4},{1,5},{2,6},{3,7},{4,0},{5,1},{6,2},{7,3},{8,12},{9,13},{10,... | collective-permute-start | bytes 393224 | tf_op jit(solution)/shard_map/ppermute | solution.py:341
  81.9 12.9 %collective-permute-start.12 = (f32[128,256]{1,0:T(8,128)S(1)}, f32[128,256]{1,0:T(8,128)S(1)}, u32[]{:S(2)}, u32[]{:S(2)}) collective-permute-start(f32[128,256]{1,0:T(8,128)S(1)} %separator.1.own_ref), channel_id=1, source_target_pairs={{0,6},{1,7},{2,4},{3,5},{4,2},{5,3},{6,0},{7,1},{8,14},{9,15},{10,... | collective-permute-start | bytes 393224 | tf_op jit(solution)/shard_map/ppermute | solution.py:341
  84.6 10.2 %collective-permute-start.8 = (f32[128,256]{1,0:T(8,128)S(1)}, f32[128,256]{1,0:T(8,128)S(1)}, u32[]{:S(2)}, u32[]{:S(2)}) collective-permute-start(f32[128,256]{1,0:T(8,128)S(1)} %separator.1.own_ref), channel_id=1, source_target_pairs={{0,2},{1,3},{2,0},{3,1},{4,6},{5,7},{6,4},{7,5},{8,10},{9,11},{10,... | collective-permute-start | bytes 393224 | tf_op jit(solution)/shard_map/ppermute | solution.py:341
  85.1 9.7 %collective-permute-start.11 = (f32[128,256]{1,0:T(8,128)S(1)}, f32[128,256]{1,0:T(8,128)S(1)}, u32[]{:S(2)}, u32[]{:S(2)}) collective-permute-start(f32[128,256]{1,0:T(8,128)S(1)} %collective-permute-done.7.far_ref), channel_id=1, source_target_pairs={{0,4},{1,5},{2,6},{3,7},{4,0},{5,1},{6,2},{7,3},{8,12},{9,13},{10,... | collective-permute-start | bytes 393224 | tf_op jit(solution)/shard_map/ppermute | solution.py:341
  86.6 8.2 %collective-permute-start.13 = (f32[128,256]{1,0:T(8,128)S(1)}, f32[128,256]{1,0:T(8,128)S(1)}, u32[]{:S(2)}, u32[]{:S(2)}) collective-permute-start(f32[128,256]{1,0:T(8,128)S(1)} %collective-permute-done.7.far_ref), channel_id=1, source_target_pairs={{0,6},{1,7},{2,4},{3,5},{4,2},{5,3},{6,0},{7,1},{8,14},{9,15},{10,... | collective-permute-start | bytes 393224 | tf_op jit(solution)/shard_map/ppermute | solution.py:341
  89.3 5.5 %collective-permute-start.9 = (f32[128,256]{1,0:T(8,128)S(1)}, f32[128,256]{1,0:T(8,128)S(1)}, u32[]{:S(2)}, u32[]{:S(2)}) collective-permute-start(f32[128,256]{1,0:T(8,128)S(1)} %collective-permute-done.7.far_ref), channel_id=1, source_target_pairs={{0,2},{1,3},{2,0},{3,1},{4,6},{5,7},{6,4},{7,5},{8,10},{9,11},{10,... | collective-permute-start | bytes 393224 | tf_op jit(solution)/shard_map/ppermute | solution.py:341
  90.4 4.5 %copy-start.1 = (f32[8,256,256]{2,1,0:T(8,128)S(1)}, f32[8,256,256]{2,1,0:T(8,128)}, u32[]{:S(2)}) copy-start(f32[8,256,256]{2,1,0:T(8,128)} %refs_10_.1) | copy-start | bytes 6291460
  90.4 4.5 %copy-start.5 = (f32[8,256]{1,0:T(8,128)S(1)}, f32[8,256]{1,0:T(8,128)}, u32[]{:S(2)}) copy-start(f32[8,256]{1,0:T(8,128)} %refs_11_.1) | copy-start | bytes 24580
  105.2 27.8 %copy-start.3 = (f32[512,512]{1,0:T(8,128)S(1)}, f32[512,512]{1,0:T(8,128)}, u32[]{:S(2)}) copy-start(f32[512,512]{1,0:T(8,128)} %all-gather.2.cloned.1.call-done.lists_ref) | copy-start | bytes 3145732
  130.4 2.7 %collective-permute-start.14 = (f32[8,256,128]{2,1,0:T(8,128)S(1)}, f32[8,256,128]{2,1,0:T(8,128)S(1)}, u32[]{:S(2)}, u32[]{:S(2)}) collective-permute-start(f32[8,256,128]{2,1,0:T(8,128)S(1)} %bitcast.14), channel_id=1, source_target_pairs={{0,8},{8,0},{1,9},{9,1},{2,10},{10,2},{3,11},{11,3},{4,12},{12,4},... | collective-permute-start | bytes 3145736 | tf_op jit(solution)/shard_map/ppermute | solution.py:375
Sparse Core Ops, SparseCore 0:
  29.1 47.3 all-gather.1
